TPU v7x, 32 devices: a whole 2x2x4 slice. The times are simulated.
32 devices in a mesh: dp: 8 (over z, y), mp: 4 (over x, core).
Axes of the slice: x: 2, y: 2, z: 4, core: 2. Of those that a mesh axis runs over, the one named last changes fastest.
Arguments:
- captions: bfloat16 [512, 16, 768], P('dp'), may hold values from -6 to 6
- token_ids: int32 [512, 16], P('dp'), may hold values from 0 to 49407, as said below
- pairing: int32 [512], P('dp'), may hold values from 0 to 511, each once
- low_images: bfloat16 [64, 50, 768], P(('dp', 'mp')), may hold values from -6 to 6
- high_images: bfloat16 [448, 145, 768], P(('dp', 'mp')), may hold values from -6 to 6
- frozen_qkv: bfloat16 [3, 768, 768], replicated, may hold values from -0.21875 to 0.21875
- frozen_out: bfloat16 [768, 768], replicated, may hold values from -1.75 to 1.75
- frozen_up: bfloat16 [768, 3072], replicated, may hold values from -0.21875 to 0.21875
- frozen_down: bfloat16 [3072, 768], replicated, may hold values from -0.109375 to 0.109375
- frozen_gains: float32 [2, 768], replicated, may hold values from 0.5 to 1.5
- master_qkv: float32 [3, 768, 768], P(None, 'dp', 'mp'), may hold values from -0.21875 to 0.21875
- master_out: float32 [768, 768], P('mp', 'dp'), may hold values from -0.625 to 0.625
- master_up: float32 [768, 3072], P('dp', 'mp'), may hold values from -0.21875 to 0.21875
- master_down: float32 [3072, 768], P('mp', 'dp'), may hold values from -0.109375 to 0.109375
- master_norms: float32 [4, 768], P(None, 'dp'), may hold values from -0.9 to 1.3, as said below
- first_qkv: float32 [3, 768, 768], P(None, 'dp', 'mp')
- first_out: float32 [768, 768], P('mp', 'dp')
- first_up: float32 [768, 3072], P('dp', 'mp')
- first_down: float32 [3072, 768], P('mp', 'dp')
- first_norms: float32 [4, 768], P(None, 'dp')
- second_qkv: float32 [3, 768, 768], P(None, 'dp', 'mp'), as said below
- second_out: float32 [768, 768], P('mp', 'dp'), as said below
- second_up: float32 [768, 3072], P('dp', 'mp'), as said below
- second_down: float32 [3072, 768], P('mp', 'dp'), as said below
- second_norms: float32 [4, 768], P(None, 'dp'), as said below
Outputs:
- input_grad: float32 [512, 16, 768], P('dp')
- grad_qkv: float32 [3, 768, 768], P(None, 'dp', 'mp')
- grad_out: float32 [768, 768], P('mp', 'dp')
- grad_up: float32 [768, 3072], P('dp', 'mp')
- grad_down: float32 [3072, 768], P('mp', 'dp')
- grad_norms: float32 [4, 768], P(None, 'dp')
- new_qkv: float32 [3, 768, 768], P(None, 'dp', 'mp')
- new_out: float32 [768, 768], P('mp', 'dp')
- new_up: float32 [768, 3072], P('dp', 'mp')
- new_down: float32 [3072, 768], P('mp', 'dp')
- new_norms: float32 [4, 768], P(None, 'dp')
- copy_qkv: bfloat16 [3, 768, 768], P(None, 'dp', 'mp')
- copy_out: bfloat16 [768, 768], P('mp', 'dp')
- copy_up: bfloat16 [768, 3072], P('dp', 'mp')
- copy_down: bfloat16 [3072, 768], P('mp', 'dp')
- copy_norms: bfloat16 [4, 768], P(None, 'dp')
- mean_qkv: float32 [3, 768, 768], P(None, 'dp', 'mp')
- mean_out: float32 [768, 768], P('mp', 'dp')
- mean_up: float32 [768, 3072], P('dp', 'mp')
- mean_down: float32 [3072, 768], P('mp', 'dp')
- mean_norms: float32 [4, 768], P(None, 'dp')
- square_qkv: float32 [3, 768, 768], P(None, 'dp', 'mp')
- square_out: float32 [768, 768], P('mp', 'dp')
- square_up: float32 [768, 3072], P('dp', 'mp')
- square_down: float32 [3072, 768], P('mp', 'dp')
- square_norms: float32 [4, 768], P(None, 'dp')
- matrix_norms: float32 [2, 10], replicated
Inputs may be any that keep to these rules, and one draw needn't show every extreme that they name: `token_ids`: each caption is a run of nonzero ids followed by zeros, with 4 to 16 nonzero ids; some caption has all 16 tokens nonzero. A permutation: caption c is paired with image pairing[c]. `master_norms`: rows 0 and 2 are gains, rows 1 and 3 shifts. `second_qkv`: every entry is positive. `second_out`: every entry is positive. `second_up`: every entry is positive. `second_down`: every entry is positive. `second_norms`: every entry is positive.
All inputs are finite; a program needn't handle non-finite values.
Results may differ from a plain program's by a relative error of at most 0.012.
The roundings to bfloat16 on the way count: a program that leaves them out, or rounds other values in their place, can miss the bound.
Values may be sent and summed in bfloat16 or wider, within the bound.
A program may use at most 192 MiB of HBM per device.

v0:
```python
from functools import partial

import jax
import jax.numpy as jnp
from jax import lax
from jax.sharding import PartitionSpec as P

HEAD_DIM = 64
STEP = 5


logit_scale = 48.0
learning_rate = 0.5
weight_decay = 0.01


def layer_norm(inputs, gain, shift):
    centre = inputs - jnp.mean(inputs, axis=-1, keepdims=True)
    spread = jnp.mean(centre * centre, axis=-1, keepdims=True)
    return centre * lax.rsqrt(spread + 1e-05) * gain + shift


def frozen_embed(rows, frozen_qkv, frozen_out, frozen_up, frozen_down, frozen_gains):
    batch_rows, seq_rows, width_all = rows.shape
    head_count = width_all // HEAD_DIM
    inputs = rows.astype(jnp.float32)
    normed = layer_norm(inputs, frozen_gains[0], 0.0).astype(jnp.bfloat16)
    projected = jnp.einsum(
        "bld,tde->tble", normed, frozen_qkv, preferred_element_type=jnp.float32
    ).astype(jnp.bfloat16)
    heads_all = projected.reshape(3, batch_rows, seq_rows, head_count, HEAD_DIM)
    scores = jnp.einsum(
        "bqhd,bkhd->bhqk", heads_all[0], heads_all[1], preferred_element_type=jnp.float32
    ) * HEAD_DIM ** (-0.5)
    weights_soft = jax.nn.softmax(scores, axis=-1).astype(jnp.bfloat16)
    context = jnp.einsum(
        "bhqk,bkhd->bqhd", weights_soft, heads_all[2], preferred_element_type=jnp.float32
    )
    context = context.reshape(batch_rows, seq_rows, width_all).astype(jnp.bfloat16)
    after_attn = inputs + jnp.einsum(
        "bld,de->ble", context, frozen_out, preferred_element_type=jnp.float32
    )
    normed_two = layer_norm(after_attn, frozen_gains[1], 0.0).astype(jnp.bfloat16)
    pre_act = jnp.einsum("bld,df->blf", normed_two, frozen_up, preferred_element_type=jnp.float32)
    hidden = jax.nn.gelu(pre_act, approximate=True).astype(jnp.bfloat16)
    outputs = after_attn + jnp.einsum(
        "blf,fd->bld", hidden, frozen_down, preferred_element_type=jnp.float32
    )
    leading = outputs[:, 0, :]
    return (leading * lax.rsqrt(jnp.sum(leading * leading, axis=1, keepdims=True) + 1e-06)).astype(
        jnp.bfloat16
    )


def lamb_parts(weight, grad, first, second, axes):
    mean_new = 0.9 * first + 0.1 * grad
    square_new = 0.999 * second + 0.001 * grad * grad
    update = (
        mean_new / (1.0 - 0.9**STEP) / (jnp.sqrt(square_new / (1.0 - 0.999**STEP)) + 1e-06)
        + weight_decay * weight
    )
    weight_sq = jnp.sum(weight * weight, axis=axes)
    update_sq = jnp.sum(update * update, axis=axes)
    return (update, mean_new, square_new, weight_sq.reshape(-1), update_sq.reshape(-1))


def shards(
    captions,
    token_ids,
    pairing,
    low_images,
    high_images,
    frozen_qkv,
    frozen_out,
    frozen_up,
    frozen_down,
    frozen_gains,
    master_qkv,
    master_out,
    master_up,
    master_down,
    master_norms,
    first_qkv,
    first_out,
    first_up,
    first_down,
    first_norms,
    second_qkv,
    second_out,
    second_up,
    second_down,
    second_norms,
):
    bf16 = jnp.bfloat16
    f32 = jnp.float32
    full_qkv, full_out, full_up, full_down, full_norms = (
        lax.all_gather(master_qkv.astype(bf16), "dp", axis=1, tiled=True),
        lax.all_gather(master_out.astype(bf16), "dp", axis=1, tiled=True),
        lax.all_gather(master_up.astype(bf16), "dp", axis=0, tiled=True),
        lax.all_gather(master_down.astype(bf16), "dp", axis=1, tiled=True),
        lax.all_gather(master_norms.astype(bf16), "dp", axis=1, tiled=True),
    )
    norm_vals = full_norms.astype(f32)
    low_embed = frozen_embed(
        low_images, frozen_qkv, frozen_out, frozen_up, frozen_down, frozen_gains
    )
    high_embed = frozen_embed(
        high_images, frozen_qkv, frozen_out, frozen_up, frozen_down, frozen_gains
    )
    local_images = jnp.concatenate([low_embed, high_embed], axis=0)
    cap_rows, seq_rows, width_all = captions.shape
    local_width = full_qkv.shape[2]
    local_heads = local_width // HEAD_DIM
    head_scale = HEAD_DIM ** (-0.5)
    inputs = captions.astype(f32)
    alive = (token_ids != 0).astype(f32)
    causal = jnp.tril(jnp.ones((seq_rows, seq_rows), dtype=jnp.bool_))
    keep_mask = causal[None, None] & (alive[:, None, None, :] > 0.5)
    normed_one = layer_norm(inputs, norm_vals[0], norm_vals[1]).astype(bf16)
    projected = jnp.einsum(
        "bld,tde->tble", normed_one, full_qkv, preferred_element_type=f32
    ).astype(bf16)
    heads_all = projected.reshape(3, cap_rows, seq_rows, local_heads, HEAD_DIM)
    query_heads, key_heads, value_heads = (heads_all[0], heads_all[1], heads_all[2])
    scores = (
        jnp.einsum("bqhd,bkhd->bhqk", query_heads, key_heads, preferred_element_type=f32)
        * head_scale
    )
    scores = jnp.where(keep_mask, scores, -1e30)
    weights_soft = jax.nn.softmax(scores, axis=-1)
    weights_low = weights_soft.astype(bf16)
    context = jnp.einsum("bhqk,bkhd->bqhd", weights_low, value_heads, preferred_element_type=f32)
    context = context.reshape(cap_rows, seq_rows, local_width).astype(bf16)
    attn_part = jnp.einsum("bld,de->ble", context, full_out, preferred_element_type=f32)
    after_attn = inputs + lax.psum(attn_part, "mp")
    normed_two = layer_norm(after_attn, norm_vals[2], norm_vals[3]).astype(bf16)
    pre_act = jnp.einsum("bld,df->blf", normed_two, full_up, preferred_element_type=f32)
    hidden = jax.nn.gelu(pre_act, approximate=True).astype(bf16)
    mlp_part = jnp.einsum("blf,fd->bld", hidden, full_down, preferred_element_type=f32)
    outputs = after_attn + lax.psum(mlp_part, "mp")
    counted = jnp.sum(alive, axis=1, keepdims=True)
    pooled = jnp.sum(outputs * alive[:, :, None], axis=1) / counted
    inverse = lax.rsqrt(jnp.sum(pooled * pooled, axis=1, keepdims=True) + 1e-06)
    unit = pooled * inverse
    text = unit.astype(bf16)
    images_all = lax.all_gather(local_images, ("dp", "mp"), axis=0, tiled=True)
    total_caps = images_all.shape[0]
    logits = logit_scale * jnp.dot(text, images_all.T, preferred_element_type=f32)
    row_top = jnp.max(logits, axis=1, keepdims=True)
    row_lse = row_top + jnp.log(jnp.sum(jnp.exp(logits - row_top), axis=1, keepdims=True))
    matched = (jnp.arange(total_caps, dtype=jnp.int32)[None, :] == pairing[:, None]).astype(f32)
    dlogits = (jnp.exp(logits - row_lse) - matched) / total_caps
    dscores = (logit_scale * dlogits).astype(bf16)
    dunit = jnp.dot(dscores, images_all, preferred_element_type=f32)
    dpooled = inverse * (dunit - unit * jnp.sum(unit * dunit, axis=1, keepdims=True))
    dout = (dpooled / counted)[:, None, :] * alive[:, :, None]
    dmlp = dout.astype(bf16)
    dhidden = jnp.einsum("bld,fd->blf", dmlp, full_down, preferred_element_type=f32)
    grad_down = jnp.einsum("blf,bld->fd", hidden, dmlp, preferred_element_type=f32)
    gelu_pull = jax.vjp(partial(jax.nn.gelu, approximate=True), pre_act)[1]
    dpre = gelu_pull(dhidden)[0].astype(bf16)
    grad_up = jnp.einsum("bld,blf->df", normed_two, dpre, preferred_element_type=f32)
    dnormed_two = lax.psum(
        jnp.einsum("blf,df->bld", dpre, full_up, preferred_element_type=f32), "mp"
    )
    ln_two_pull = jax.vjp(layer_norm, after_attn, norm_vals[2], norm_vals[3])[1]
    dafter_ln, dgain_two, dshift_two = ln_two_pull(dnormed_two)
    dafter = dout + dafter_ln
    dattn = dafter.astype(bf16)
    grad_out = jnp.einsum("bld,ble->de", context, dattn, preferred_element_type=f32)
    dcontext = jnp.einsum("ble,de->bld", dattn, full_out, preferred_element_type=f32).astype(bf16)
    dcontext = dcontext.reshape(cap_rows, seq_rows, local_heads, HEAD_DIM)
    dweights = jnp.einsum("bqhd,bkhd->bhqk", dcontext, value_heads, preferred_element_type=f32)
    dlogit_attn = weights_soft * (
        dweights - jnp.sum(weights_soft * dweights, axis=-1, keepdims=True)
    )
    dlogit_low = dlogit_attn.astype(bf16)
    dquery = (
        jnp.einsum("bhqk,bkhd->bqhd", dlogit_low, key_heads, preferred_element_type=f32)
        * head_scale
    ).astype(bf16)
    dkey = (
        jnp.einsum("bhqk,bqhd->bkhd", dlogit_low, query_heads, preferred_element_type=f32)
        * head_scale
    ).astype(bf16)
    dvalue = jnp.einsum(
        "bhqk,bqhd->bkhd", weights_low, dcontext, preferred_element_type=f32
    ).astype(bf16)
    dprojected = jnp.stack([dquery, dkey, dvalue]).reshape(3, cap_rows, seq_rows, local_width)
    grad_qkv = jnp.einsum("bld,tble->tde", normed_one, dprojected, preferred_element_type=f32)
    dnormed_one = lax.psum(
        jnp.einsum("tble,tde->bld", dprojected, full_qkv, preferred_element_type=f32), "mp"
    )
    ln_one_pull = jax.vjp(layer_norm, inputs, norm_vals[0], norm_vals[1])[1]
    dinput_ln, dgain_one, dshift_one = ln_one_pull(dnormed_one)
    input_grad = dafter + dinput_ln
    grad_norms_local = jnp.stack([dgain_one, dshift_one, dgain_two, dshift_two])
    local_grads = (grad_qkv, grad_out, grad_up, grad_down, grad_norms_local)
    masters = (master_qkv, master_out, master_up, master_down, master_norms)
    slice_dims = (1, 1, 0, 1, 1)
    summed = lax.psum(
        (local_grads[0], local_grads[1], local_grads[2], local_grads[3], local_grads[4]), "dp"
    )
    dp_index = lax.axis_index("dp")
    shard_grads = tuple(
        (
            lax.dynamic_slice_in_dim(
                summed[index],
                dp_index * masters[index].shape[slice_dims[index]],
                masters[index].shape[slice_dims[index]],
                slice_dims[index],
            )
            for index in range(5)
        )
    )
    firsts = (first_qkv, first_out, first_up, first_down, first_norms)
    seconds = (second_qkv, second_out, second_up, second_down, second_norms)
    axes_all = ((1, 2), (0, 1), (0, 1), (0, 1), (1,))
    parts = [
        lamb_parts(
            masters[index], shard_grads[index], firsts[index], seconds[index], axes_all[index]
        )
        for index in range(5)
    ]
    lead_flag = (lax.axis_index("mp") == 0).astype(f32)
    weight_squares = jnp.concatenate(
        [parts[0][3], parts[1][3], parts[2][3], parts[3][3], parts[4][3] * lead_flag]
    )
    update_squares = jnp.concatenate(
        [parts[0][4], parts[1][4], parts[2][4], parts[3][4], parts[4][4] * lead_flag]
    )
    total_squares = lax.psum(jnp.stack([weight_squares, update_squares]), ("dp", "mp"))
    matrix_norms = jnp.sqrt(total_squares)
    ratios = matrix_norms[0] / matrix_norms[1]
    ratio_pieces = (
        ratios[0:3].reshape(3, 1, 1),
        ratios[3],
        ratios[4],
        ratios[5],
        ratios[6:10].reshape(4, 1),
    )
    news = [
        masters[index] - learning_rate * ratio_pieces[index] * parts[index][0] for index in range(5)
    ]
    copies = [fresh.astype(bf16) for fresh in news]
    return (
        input_grad,
        shard_grads[0],
        shard_grads[1],
        shard_grads[2],
        shard_grads[3],
        shard_grads[4],
        news[0],
        news[1],
        news[2],
        news[3],
        news[4],
        copies[0],
        copies[1],
        copies[2],
        copies[3],
        copies[4],
        parts[0][1],
        parts[1][1],
        parts[2][1],
        parts[3][1],
        parts[4][1],
        parts[0][2],
        parts[1][2],
        parts[2][2],
        parts[3][2],
        parts[4][2],
        matrix_norms,
    )


def solution(mesh):
    return jax.shard_map(
        shards,
        mesh=mesh,
        in_specs=(
            P("dp", None, None),
            P("dp", None),
            P("dp"),
            P(("dp", "mp"), None, None),
            P(("dp", "mp"), None, None),
            P(),
            P(),
            P(),
            P(),
            P(),
            P(None, "dp", "mp"),
            P("mp", "dp"),
            P("dp", "mp"),
            P("mp", "dp"),
            P(None, "dp"),
            P(None, "dp", "mp"),
            P("mp", "dp"),
            P("dp", "mp"),
            P("mp", "dp"),
            P(None, "dp"),
            P(None, "dp", "mp"),
            P("mp", "dp"),
            P("dp", "mp"),
            P("mp", "dp"),
            P(None, "dp"),
        ),
        out_specs=(
            P("dp", None, None),
            P(None, "dp", "mp"),
            P("mp", "dp"),
            P("dp", "mp"),
            P("mp", "dp"),
            P(None, "dp"),
            P(None, "dp", "mp"),
            P("mp", "dp"),
            P("dp", "mp"),
            P("mp", "dp"),
            P(None, "dp"),
            P(None, "dp", "mp"),
            P("mp", "dp"),
            P("dp", "mp"),
            P("mp", "dp"),
            P(None, "dp"),
            P(None, "dp", "mp"),
            P("mp", "dp"),
            P("dp", "mp"),
            P("mp", "dp"),
            P(None, "dp"),
            P(None, "dp", "mp"),
            P("mp", "dp"),
            P("dp", "mp"),
            P("mp", "dp"),
            P(None, "dp"),
            P(),
        ),
        check_vma=False,
    )
```

profile of v0, /device:TPU:0, one launch (start us, length us, event | category | flops | bytes accessed | tf_op | source)
XLA Modules:
  0.0 883.0 jit_solution(531891667713521386)
XLA Ops:
  15.0 22.3 %all-gather = bf16[8,96,4]{1,2,0:T(4,128)(2,1)S(1)} all-gather(bf16[1,96,4]{1,2,0:T(4,128)(2,1)S(1)} %get-tuple-element.203), channel_id=1, replica_groups=mesh['dp'=8,'mp'=4] {'dp'}, dimensions={0}, use_global_device_ids=true | all-gather | bytes 6912 | tf_op jit(solution)/shard_map/all_gather | solution.py:101
  41.2 33.8 %all_gather.19 = bf16[3,768,192]{2,1,0:T(8,128)(2,1)S(1)} all-gather(bf16[3,96,192]{2,1,0:T(8,128)(2,1)S(1)} %get-tuple-element.199), channel_id=1, replica_groups=mesh['dp'=8,'mp'=4] {'dp'}, dimensions={1}, use_global_device_ids=true | all-gather | bytes 995328 | tf_op jit(solution)/shard_map/all_gather | solution.py:97
  110.6 31.2 %all_gather.20 = bf16[192,768]{0,1:T(8,128)(2,1)S(1)} all-gather(bf16[192,96]{0,1:T(8,128)(2,1)} %copy.213), channel_id=1, replica_groups=mesh['dp'=8,'mp'=4] {'dp'}, dimensions={1}, use_global_device_ids=true | all-gather | bytes 331776 | tf_op jit(solution)/shard_map/all_gather | solution.py:98
  166.8 8.6 convert_bitcast_fusion
  178.6 6.5 copy.228
  185.1 6.5 copy.229
  191.6 4.2 copy.227
  195.8 17.5 %fusion.208 = (f32[14,12,145]{2,1,0:T(8,128)S(1)}, f32[14,12,145,145]{2,3,1,0:T(8,128)}) fusion(bf16[14,145,12,64]{1,3,2,0:T(8,128)(2,1)} %bitcast.190, bf16[14,145,12,64]{1,3,2,0:T(8,128)(2,1)} %bitcast.191), kind=kOutput, calls=%fused_computation.308 | convolution fusion | flops 462718336 | bytes 20462400 | tf_op jit(solution)/shard_map/sub | solution.py:35
  213.4 15.0 %fusion.54 = bf16[14,12,64,145]{3,2,1,0:T(8,128)(2,1)} fusion(bf16[14,145,12,64]{1,3,2,0:T(8,128)(2,1)} %bitcast.192, f32[14,12,145,145]{2,3,1,0:T(8,128)} %get-tuple-element.210, f32[14,12,145]{2,1,0:T(8,128)S(1)} %get-tuple-element.209), kind=kOutput, calls=%fused_computation.62 | convolution fusion | flops 460745024 | bytes 20462400 | tf_op jit(solution)/shard_map/bhqk,bkhd->bqhd/dot_general | solution.py:36
  228.4 15.7 %fusion.209 = (f32[14,145]{1,0:T(8,128)S(1)}, f32[14,145,768]{2,1,0:T(8,128)S(1)}) fusion(bf16[14,145,768]{1,2,0:T(8,128)(2,1)} %bitcast.205, bf16[768,768]{1,0:T(8,128)(2,1)} %param.31, bf16[14,145,768]{2,1,0:T(8,128)(2,1)S(1)} %copy-done.6), kind=kOutput, calls=%fused_computation.309 | convolution fusion | flops 2399360512 | bytes 13660088 | tf_op jit(solution)/shard_map/bld,de->ble/dot_general | solution.py:40
  249.9 30.3 %fusion.16 = f32[14,145,768]{2,1,0:T(8,128)} fusion(bf16[3072,768]{1,0:T(8,128)(2,1)} %param.33, bf16[768,3072]{1,0:T(8,128)(2,1)} %param.32, f32[14,145,768]{2,1,0:T(8,128)} %copy-done.8, f32[768]{0:T(1024)S(1)} %get-tuple-element.151, f32[14,145]{1,0:T(8,128)S(1)} %add_rsqrt_fusion, f32[14,145]{1,0:T(8,128)S(1)} %broadcast_multiply_fusion.2), kind=kOutput, calls=%fused_computation.18 | convolution fusion | flops 19219845120 | bytes 21928816 | tf_op jit(solution)/shard_map/blf,fd->bld/dot_general | solution.py:46
  280.2 5.6 fusion.28
  290.7 4.5 fusion.119
  295.3 5.9 fusion.115
  302.2 44.4 %all_gather.23 = bf16[512,768]{1,0:T(8,128)(2,1)} all-gather(bf16[16,768]{1,0:T(8,128)(2,1)S(1)} %pad_maximum_fusion.3), channel_id=1, replica_groups=mesh['dp'=8,'mp'=4] {'dp','mp'}, dimensions={0}, use_global_device_ids=true | all-gather | bytes 811008 | tf_op jit(solution)/shard_map/all_gather | solution.py:146
  346.6 27.9 %all-reduce.9.cloned.1.call-done = f32[64,16,768]{2,1,0:T(8,128)} async-done(((f32[64,16,768]{2,1,0:T(8,128)}), f32[64,16,768]{2,1,0:T(8,128)}) %all-reduce.9.cloned.1.call-update) | async-done | bytes 3145744 | tf_op jit(solution)/shard_map/psum | solution.py:140
  390.6 4.7 convolution_bitcast_fusion.1
  395.3 63.3 %all-reduce.11.cloned.1.call-done = f32[64,16,768]{2,1,0:T(8,128)} async-done(((f32[64,16,768]{2,1,0:T(8,128)}), f32[64,16,768]{2,1,0:T(8,128)}) %all-reduce.11.cloned.1.call-update) | async-done | bytes 3145744 | tf_op jit(solution)/shard_map/psum | solution.py:163
  483.2 4.3 convolution_bitcast_fusion
  497.7 58.6 %all-reduce.13.cloned.1.call-done = f32[64,16,768]{2,1,0:T(8,128)} async-done(((f32[64,16,768]{2,1,0:T(8,128)}), f32[64,16,768]{2,1,0:T(8,128)}) %all-reduce.13.cloned.1.call-update) | async-done | bytes 3145744 | tf_op jit(solution)/shard_map/psum | solution.py:191
  561.7 39.3 %psum.78 = f32[4,768]{1,0:T(4,128)S(1)} all-reduce(f32[4,768]{1,0:T(4,128)S(1)} %pad_maximum_fusion.4), channel_id=1, replica_groups=mesh['dp'=8,'mp'=4] {'dp'}, use_global_device_ids=true, to_apply=%region_43.44 | all-reduce | flops 3072 | bytes 24576 | tf_op jit(solution)/shard_map/psum | solution.py:201
  603.1 194.0 %all-reduce.15.cloned.1.call-done = (f32[3,768,192]{1,2,0:T(8,128)}, f32[192,768]{1,0:T(8,128)}, f32[768,768]{1,0:T(8,128)}, f32[768,768]{0,1:T(8,128)}) async-done(((f32[3,768,192]{1,2,0:T(8,128)}, f32[192,768]{1,0:T(8,128)}, f32[768,768]{1,0:T(8,128)}, f32[768,768]{0,1:T(8,128)}), (f32[3,768,192]{1,2,0:T(8,128)}, f32[192,768]{1,0:T(8,128)}, f32[768,768]{1,0:T(8,128)}, ...) | async-done | bytes 7077904 | tf_op jit(solution)/shard_map/psum | solution.py:201
  811.2 4.7 add_add_fusion.2
  816.0 39.1 %psum.79 = f32[2,10]{1,0:T(2,128)S(1)} all-reduce(f32[2,10]{1,0:T(2,128)S(1)} %pad_maximum_fusion.5), channel_id=1, replica_groups=mesh['dp'=8,'mp'=4] {'dp','mp'}, use_global_device_ids=true, to_apply=%region_54.55 | all-reduce | flops 20 | bytes 160 | tf_op jit(solution)/shard_map/psum | solution.py:232
  (317 shorter events, 176.6 us)
Async XLA Ops:
  8.0 143.8 %copy-start = (bf16[3,768,768]{2,1,0:T(8,128)(2,1)S(1)}, bf16[3,768,768]{2,1,0:T(8,128)(2,1)}, u32[]{:S(2)}) copy-start(bf16[3,768,768]{2,1,0:T(8,128)(2,1)} %param.30) | copy-start | bytes 10616836
  8.1 279.2 %all-reduce.7.cloned.1.call-start = ((), (), s32[]{:S(2)}) async-start(), calls=%async_computation | async-start | bytes 6291456 | tf_op jit(solution)/shard_map/psum | solution.py:135
  39.4 39.1 %copy-start.54 = (f32[768]{0:T(1024)}, f32[768]{0:T(1024)S(1)}, u32[]{:S(2)}) copy-start(f32[768]{0:T(1024)S(1)} %get-tuple-element.150) | copy-start | bytes 9220
  39.4 39.1 %copy-start.64 = (f32[768]{0:T(1024)}, f32[768]{0:T(1024)S(1)}, u32[]{:S(2)}) copy-start(f32[768]{0:T(1024)S(1)} %get-tuple-element.149) | copy-start | bytes 9220
  145.9 144.7 %all-gather.4.cloned.1.call-start = ((), (), s32[]{:S(2)}) async-start(), calls=%async_computation.1 | async-start | bytes 1327104 | tf_op jit(solution)/shard_map/all_gather | solution.py:99
  147.6 147.7 %all-gather.6.cloned.1.call-start = ((), (), s32[]{:S(2)}) async-start(), calls=%async_computation.2 | async-start | bytes 1327104 | tf_op jit(solution)/shard_map/all_gather | solution.py:100
  149.3 225.2 %all-reduce.9.cloned.1.call-start = ((), (), s32[]{:S(2)}) async-start(), calls=%async_computation.3 | async-start | bytes 6291456 | tf_op jit(solution)/shard_map/psum | solution.py:140
  286.0 88.5 %copy-start.34 = (f32[64,16]{1,0:T(8,128)}, f32[64,16]{1,0:T(8,128)S(1)}, u32[]{:S(2)}) copy-start(f32[64,16]{1,0:T(8,128)S(1)} %copy.216) | copy-start | bytes 12292
  301.2 157.3 %all-reduce.11.cloned.1.call-start = ((), (), s32[]{:S(2)}) async-start(), calls=%async_computation.4 | async-start | bytes 6291456 | tf_op jit(solution)/shard_map/psum | solution.py:163
  346.6 31.6 %copy-start.76 = (s32[64]{0:T(128)S(1)}, s32[64]{0:T(128)}, u32[]{:S(2)}) copy-start(s32[64]{0:T(128)} %param.27) | copy-start | bytes 772
  389.9 166.5 %all-reduce.13.cloned.1.call-start = ((), (), s32[]{:S(2)}) async-start(), calls=%async_computation.5 | async-start | bytes 6291456 | tf_op jit(solution)/shard_map/psum | solution.py:191
  395.3 66.3 %copy-start.47 = (f32[64,16]{1,0:T(8,128)S(1)}, f32[64,16]{1,0:T(8,128)}, u32[]{:S(2)}) copy-start(f32[64,16]{1,0:T(8,128)} %copy-done.46) | copy-start | bytes 12292
  487.7 309.4 %all-reduce.15.cloned.1.call-start = ((), (), s32[]{:S(2)}) async-start(), calls=%async_computation.6 | async-start | bytes 14155776 | tf_op jit(solution)/shard_map/psum | solution.py:201
  495.9 309.1 %copy-start.13 = (f32[3,96,192]{1,2,0:T(8,128)}, f32[3,96,192]{1,2,0:T(8,128)S(1)}, u32[]{:S(2)}) copy-start(f32[3,96,192]{1,2,0:T(8,128)S(1)} %copy.252) | copy-start | bytes 663556
  495.9 63.2 %copy-start.49 = (f32[64,16]{1,0:T(8,128)S(1)}, f32[64,16]{1,0:T(8,128)}, u32[]{:S(2)}) copy-start(f32[64,16]{1,0:T(8,128)} %copy-done.48) | copy-start | bytes 12292
  559.1 42.0 %copy-start.61 = (f32[4,96]{1,0:T(4,128)S(1)}, f32[4,96]{1,0:T(4,128)}, u32[]{:S(2)}) copy-start(f32[4,96]{1,0:T(4,128)} %param.39) | copy-start | bytes 4612
  559.1 238.0 %copy-start.16 = (f32[96,768]{1,0:T(8,128)S(1)}, f32[96,768]{1,0:T(8,128)}, u32[]{:S(2)}) copy-start(f32[96,768]{1,0:T(8,128)} %param.37) | copy-start | bytes 884740
  559.2 41.9 %copy-start.67 = (f32[4,96]{1,0:T(4,128)S(1)}, f32[4,96]{1,0:T(4,128)}, u32[]{:S(2)}) copy-start(f32[4,96]{1,0:T(4,128)} %param.44) | copy-start | bytes 4612
  559.2 41.9 %copy-start.68 = (f32[4,96]{1,0:T(4,128)S(1)}, f32[4,96]{1,0:T(4,128)}, u32[]{:S(2)}) copy-start(f32[4,96]{1,0:T(4,128)} %param.49) | copy-start | bytes 4612
  559.2 240.7 %copy-start.15 = (f32[768,96]{0,1:T(8,128)S(1)}, f32[768,96]{0,1:T(8,128)}, u32[]{:S(2)}) copy-start(f32[768,96]{0,1:T(8,128)} %param.38) | copy-start | bytes 884740
  561.7 240.9 %copy-start.26 = (f32[192,96]{1,0:T(8,128)S(1)}, f32[192,96]{1,0:T(8,128)}, u32[]{:S(2)}) copy-start(f32[192,96]{1,0:T(8,128)} %param.36) | copy-start | bytes 221188
  807.1 51.1 %copy-start.14 = (f32[3,96,192]{1,2,0:T(8,128)}, f32[3,96,192]{1,2,0:T(8,128)S(1)}, u32[]{:S(2)}) copy-start(f32[3,96,192]{1,2,0:T(8,128)S(1)} %get-tuple-element.182) | copy-start | bytes 663556
  855.1 18.8 %copy-start.70 = (f32[2,10]{1,0:T(2,128)}, f32[2,10]{1,0:T(2,128)S(1)}, u32[]{:S(2)}) copy-start(f32[2,10]{1,0:T(2,128)S(1)} %sqrt.23) | copy-start | bytes 244
  859.1 16.5 %copy-start.1 = (bf16[3,768,768]{2,1,0:T(8,128)(2,1)S(1)}, bf16[3,768,768]{2,1,0:T(8,128)(2,1)}, u32[]{:S(2)}) copy-start(bf16[3,768,768]{2,1,0:T(8,128)(2,1)} %param.30) | copy-start | bytes 10616836
  (63 other events, 220.2 us)
Sparse Core Ops, SparseCore 0:
  146.0 66.8 all-reduce.6
  301.3 73.1 all-reduce.8
  390.0 68.5 all-reduce.10
  487.8 68.5 all-reduce.12
  560.6 236.4 all-reduce.14
Sparse Core Ops, SparseCore 1:
  149.1 39.8 all-gather.3
  191.6 39.9 all-gather.5
where the time goes:
time: 888 us; the launch traced here: 883 us
  waiting for transfers between devices  344 us (39%)
  blocking collectives  210 us (24%)
  matrix products  157 us (18%)
  local copies, waits for them, and re-layouts  88.1 us (10%)
  other arithmetic  65 us (7%)
  between operations  18.4 us (2%)
    psum x1, waiting for transfers between devices, shards(): lax.psum((local_grads[0], local_grads[1], local_grads[2], local_grads[3],...  194 us
    psum x1, waiting for transfers between devices, shards(): lax.psum(jnp.einsum('blf,df->bld', dpre, full_up, preferred_element_type=...  63.3 us
    psum x1, waiting for transfers between devices, shards(): lax.psum(jnp.einsum('tble,tde->bld', dprojected, full_qkv, preferred_elem...  58.6 us
    all_gather x1, blocking collectives, shards(): images_all = lax.all_gather(local_images, ('dp', 'mp'), axis=0, tiled=True)  44.4 us
    psum x1, blocking collectives, shards(): lax.psum((local_grads[0], local_grads[1], local_grads[2], local_grads[3],...  39.3 us
    psum x1, blocking collectives, shards(): lax.psum(jnp.stack([weight_squares, update_squares]), ('dp', 'mp'))  39.1 us
    dot_general x2, matrix products, frozen_embed(): jnp.einsum('blf,fd->bld', hidden, frozen_down, preferred_element_type=jnp...  35.9 us
    all_gather x1, blocking collectives, shards(): lax.all_gather(master_qkv.astype(bf16), 'dp', axis=1, tiled=True)  33.8 us
  transfers between devices with their start and end apart: 7, of which 4 were waited for; matrix products, arithmetic and copies ran while one was open for 19% of the time, Pallas kernels for 0%

commit v1 on v0

--- a/solution.py
+++ b/solution.py
@@ -1,8 +1,11 @@
 from functools import partial
+from types import SimpleNamespace
 
 import jax
 import jax.numpy as jnp
 from jax import lax
+from jax.experimental import pallas as pl
+from jax.experimental.pallas import tpu as pltpu
 from jax.sharding import PartitionSpec as P
 
 HEAD_DIM = 64
@@ -274,9 +277,1107 @@
     )
 
 
+MESH = pl.DeviceIdType.MESH
+BF = jnp.bfloat16
+F32 = jnp.float32
+HIGHEST = lax.Precision.HIGHEST
+
+
+def nn(a, b):
+    return lax.dot_general(a, b, (((1,), (0,)), ((), ())), preferred_element_type=F32)
+
+
+def nt(a, b):
+    return lax.dot_general(a, b, (((1,), (1,)), ((), ())), preferred_element_type=F32)
+
+
+def tn(a, b):
+    return lax.dot_general(a, b, (((0,), (0,)), ((), ())), preferred_element_type=F32)
+
+
+def iota(shape, dim):
+    return lax.broadcasted_iota(jnp.int32, shape, dim)
+
+
+def stats(values):
+    centre = values - jnp.mean(values, axis=-1, keepdims=True)
+    return centre, lax.rsqrt(jnp.mean(centre * centre, axis=-1, keepdims=True) + 1e-05)
+
+
+def gelu_pair(u):
+    root = 0.7978845608028654
+    square = u * u
+    t = jnp.tanh(root * (u + 0.044715 * square * u))
+    half = 0.5 * (1.0 + t)
+    slope = half + 0.5 * u * (1.0 - t * t) * (root * (1.0 + 3.0 * 0.044715 * square))
+    return u * half, slope
+
+
+def gelu_only(u):
+    root = 0.7978845608028654
+    return 0.5 * u * (1.0 + jnp.tanh(root * (u + 0.044715 * u * u * u)))
+
+
+def pack_attn(qkv_ref, out_ref):
+    q, k, v = qkv_ref[0], qkv_ref[1], qkv_ref[2]
+    out_t = out_ref[...].T
+    return [
+        q[:, 0:128],
+        k[:, 0:128],
+        v[:, 0:128],
+        jnp.concatenate([q[:, 128:192], v[:, 128:192]], axis=1),
+        jnp.concatenate([k[:, 128:192], out_t[:, 128:192]], axis=1),
+        out_t[:, 0:128],
+    ]
+
+
+def lamb_update(weight, grad, first, second):
+    mean_new = 0.9 * first + 0.1 * grad
+    square_new = 0.999 * second + 0.001 * grad * grad
+    update = (
+        mean_new * (1.0 / (1.0 - 0.9**STEP))
+        / (jnp.sqrt(square_new * (1.0 / (1.0 - 0.999**STEP))) + 1e-06)
+        + weight_decay * weight
+    )
+    return update, mean_new, square_new
+
+
+CHUNKS = 4
+
+
+def scratch_table():
+    vm = pltpu.VMEM
+    dma = pltpu.SemaphoreType.DMA
+    return dict(
+        cap=vm((1024, 768), BF),
+        tok=vm((16, 64), jnp.int32),
+        pair=vm((1, 64), jnp.int32),
+        alive=vm((8, 128), F32),
+        pair_v=vm((64, 1), F32),
+        fg_v=vm((2, 768), F32),
+        qkv_v=vm((3, 96, 192), F32),
+        out_v=vm((192, 96), F32),
+        up_v=vm((96, 768), F32),
+        down_v=vm((96, 768), F32),
+        norms_v=vm((4, 96), F32),
+        fin_v=vm((4, 96), F32),
+        sen_v=vm((4, 96), F32),
+        gsh=vm((3, 96, 768), F32),
+        gn=vm((8, 128), F32),
+        tot=vm((8, 128), F32),
+        w=vm((3, 768, 768), BF),
+        ns=vm((16, 128), F32),
+        nsend=vm((16, 128), BF),
+        nslot=vm((8, 16, 128), BF),
+        normp=vm((16, 768), F32),
+        mu=vm((1024, 1), F32),
+        rs=vm((1024, 1), F32),
+        causal=vm((128, 128), F32),
+        n1=vm((1024, 768), BF),
+        proj=vm((1024, 640), BF),
+        p=vm((8, 3, 128, 128), F32),
+        o=vm((1024, 256), BF),
+        part=vm((1024, 768), F32),
+        cs=vm((CHUNKS, 128, 768), BF),
+        cr1=vm((CHUNKS, 128, 768), BF),
+        cr2=vm((CHUNKS, 128, 768), BF),
+        xs=vm((CHUNKS, 128, 768), BF),
+        xr1=vm((CHUNKS, 128, 768), BF),
+        xr2=vm((CHUNKS, 128, 768), BF),
+        a=vm((CHUNKS, 128, 768), F32),
+        n2=vm((1024, 768), BF),
+        gp=vm((1024, 768), F32),
+        hs=vm((2, 32, 768), F32),
+        hl=vm((128, 768), BF),
+        asum=vm((32, 768), F32),
+        cnt=vm((32, 128), F32),
+        pp=vm((2, 32, 768), F32),
+        pcr=vm((32, 768), F32),
+        pxs=vm((32, 768), F32),
+        pxr=vm((32, 768), F32),
+        emb=vm((4, 2, 4, 16, 768), BF),
+        dy=vm((2, 32, 768), BF),
+        dpc=vm((32, 768), F32),
+        dh=vm((2, 32, 768), F32),
+        dz=vm((1024, 768), BF),
+        rss=vm((3, 2, 7, 48, 768), BF),
+        rsr=vm((3, 2, 7, 48, 768), BF),
+        gns=vm((8, 768), F32),
+        gnr=vm((8, 768), F32),
+        gsl=vm((8, 8, 128), F32),
+        gslr=vm((9, 8, 128), F32),
+        sqd=vm((8, 8, 128), F32),
+        sqm=vm((4, 8, 128), F32),
+        loc=dma((15,)),
+        first=dma((10,)),
+        fin=dma((5,)),
+        nsem=dma((8,)),
+        ags=dma((3,)),
+        agr=dma((3, 2, 7)),
+        rsa=dma((3,)),
+        rsb=dma((3, 2, 7)),
+        arcs=dma((CHUNKS,)),
+        arcr=dma((3, CHUNKS)),
+        arxs=dma((CHUNKS,)),
+        arxr=dma((3, CHUNKS)),
+        shs=dma((3,)),
+        shr=dma((3, CHUNKS)),
+        pos=dma((3,)),
+        por=dma((3,)),
+        ems=dma((5,)),
+        emr=dma((7,)),
+        gss=dma((3,)),
+        gsr=dma((9,)),
+        sqs=dma((2,)),
+        sqr=dma((10,)),
+        outs=dma((CHUNKS,)),
+    )
+
+
+def step_kernel(names, total_caps, *refs):
+    r = SimpleNamespace(**dict(zip(names, refs)))
+    dp = lax.axis_index("dp")
+    mp = lax.axis_index("mp")
+    z, y = dp // 2, dp % 2
+    x, c = mp // 2, mp % 2
+    sib = (dp, x * 2 + (1 - c))
+    xnb = (dp, (1 - x) * 2 + c)
+    diag = (dp, (1 - x) * 2 + (1 - c))
+    ynb = (z * 2 + (1 - y), mp)
+    place_on_ring = z + y * (7 - 2 * z)
+
+    def ring(k):
+        q = (place_on_ring + k + 8) % 8
+        return (q + (q // 4) * (7 - 2 * q)) * 2 + q // 4
+
+    ways = ((ring(1), mp), (ring(-1), mp))
+    zpeer = {k: (((z + k) % 4) * 2 + y, mp) for k in (1, 2, 3)}
+    dpeer = {k: ((dp + k) % 8, mp) for k in range(1, 8)}
+
+    def rcopy(src, dst, ssem, rsem, dev):
+        return pltpu.make_async_remote_copy(
+            src_ref=src, dst_ref=dst, send_sem=ssem, recv_sem=rsem,
+            device_id=dev, device_id_type=MESH,
+        )
+
+    sends = []
+
+    def go(make, at_end=True):
+        copy = make()
+        copy.start()
+        if at_end:
+            sends.append(make)
+        return copy
+
+    w = r.w
+
+    def shard_rows(zz, yy):
+        return pl.ds(pl.multiple_of((zz * 2 + yy) * 96, 96), 96)
+
+    def own_rows(k):
+        return pl.ds(pl.multiple_of(256 * k + 128 * c, 128), 128)
+
+    def sib_rows(k):
+        return pl.ds(pl.multiple_of(256 * k + 128 * (1 - c), 128), 128)
+
+    firsts = [
+        pltpu.make_async_copy(source, target, r.first.at[n])
+        for n, (source, target) in enumerate(
+            (
+                (r.mq_h, r.qkv_v), (r.mo_h, r.out_v), (r.mn_h, r.norms_v), (r.mu_h, r.up_v),
+                (r.md_h, r.down_v), (r.fg_h, r.fg_v), (r.tok_h, r.tok), (r.pair_h, r.pair),
+                (r.fin_h, r.fin_v), (r.sen_h, r.sen_v),
+            )
+        )
+    ]
+    for copy in firsts:
+        copy.start()
+    cap_copy = pltpu.make_async_copy(r.cap_h, r.cap, r.loc.at[0])
+    cap_copy.start()
+
+    def piece(k, half):
+        return pl.ds(pl.multiple_of(ring(k) * 96 + 48 * half, 16), 48)
+
+    def ag_copy(kind, way, step, half, k):
+        rows = w.at[kind, piece(k, half)]
+        index = min(2 * step + half, 6)
+        return rcopy(rows, rows, r.ags.at[kind], r.agr.at[kind, way, index], ways[way])
+
+    def ag_own(kind, way):
+        for half in (0, 1):
+            go(partial(ag_copy, kind, way, 0, half, 0), False)
+
+    def ag_step(kind, step, half):
+        for way in (0, 1):
+            if step == 3 and way != half:
+                continue
+            k = -step if way == 0 else step
+            ag_copy(kind, way, step - 1, half, k).wait_recv()
+            go(partial(ag_copy, kind, way, step, half, k), False)
+
+    def ag_done(kind):
+        ag_copy(kind, 0, 2, 1, -3).wait_recv()
+        ag_copy(kind, 1, 2, 0, 3).wait_recv()
+        ag_copy(kind, 0, 3, 0, -4).wait_recv()
+        ag_copy(kind, 1, 3, 1, 4).wait_recv()
+
+    def core_copy(which, k, received):
+        return rcopy(r.cs.at[k], received.at[k], r.arcs.at[k], r.arcr.at[which, k], sib)
+
+    def x_copy(which, k, received_x):
+        return rcopy(r.xs.at[k], received_x.at[k], r.arxs.at[k], r.arxr.at[which, k], xnb)
+
+    def ar_start(which, k, received):
+        if which > 0:
+            core_copy(which - 1, k, received).wait_send()
+        r.cs[k] = r.part[sib_rows(k), :].astype(BF)
+        go(lambda: core_copy(which, k, received), which == 2)
+
+    def ar_mid(which, k, received, received_x):
+        core_copy(which, k, received).wait_recv()
+        if which > 0:
+            x_copy(which - 1, k, received_x).wait_send()
+        r.xs[k] = (r.part[own_rows(k), :] + received[k].astype(F32)).astype(BF)
+        go(lambda: x_copy(which, k, received_x), which == 2)
+
+    def ar_end(which, k, received_x):
+        x_copy(which, k, received_x).wait_recv()
+        return r.xs[k].astype(F32) + received_x[k].astype(F32)
+
+    def share_copy(which, k, ref, rows):
+        part = ref.at[rows(k)]
+        return rcopy(part, part, r.shs.at[which], r.shr.at[which, k], sib)
+
+    def share(which, k, ref):
+        go(lambda: share_copy(which, k, ref, own_rows), False)
+
+    def share_wait(which, k, ref):
+        share_copy(which, k, ref, sib_rows).wait_recv()
+
+    barrier = pltpu.get_barrier_semaphore()
+    partners = [sib, xnb, diag] + [dpeer[k] for k in range(1, 8)]
+    for dev in partners:
+        pl.semaphore_signal(barrier, inc=1, device_id=dev, device_id_type=MESH)
+    for copy in firsts[0:3]:
+        copy.wait()
+    tiles = pack_attn(r.qkv_v, r.out_v)
+    mine = shard_rows(z, y)
+    for t in range(6):
+        w[0, mine, 128 * t : 128 * (t + 1)] = tiles[t].astype(BF)
+    r.ns[...] = jnp.zeros((16, 128), F32)
+    r.ns[0:4, 0:96] = r.norms_v[...]
+    r.nsend[...] = r.ns[...].astype(BF)
+    r.nslot[dp] = r.nsend[...]
+
+    pl.semaphore_wait(barrier, len(partners))
+
+    def norm_copy(k, source):
+        return rcopy(
+            r.nsend, r.nslot.at[source()], r.nsem.at[7], r.nsem.at[k - 1], dpeer[k]
+        )
+
+    for k in range(1, 8):
+        go(partial(norm_copy, k, lambda: dp), False)
+    for way in (0, 1):
+        ag_own(0, way)
+    for copy in firsts[3:10]:
+        copy.wait()
+    w[1, mine, :] = r.up_v[...].astype(BF)
+    w[2, mine, :] = r.down_v[...].astype(BF)
+
+    live = jnp.where(r.tok[...] != 0, 1.0, 0.0).astype(BF)
+    spread_caps = jnp.where(iota((64, 1024), 1) // 16 == iota((64, 1024), 0), 1.0, 0.0).astype(BF)
+    live_all = nn(live, spread_caps)
+    live_row = jnp.sum(
+        jnp.where(iota((16, 1024), 1) % 16 == iota((16, 1024), 0), live_all, 0.0), axis=0, keepdims=True
+    )
+    for b in range(8):
+        r.alive[b : b + 1, :] = live_row[:, 128 * b : 128 * (b + 1)]
+    image = r.pair[...]
+    owner_dp = image // 64
+    column = ((((image // 16) % 4) * 2 + owner_dp % 2) * 4 + owner_dp // 2) * 16 + image % 16
+    order = iota((64, 64), 0)
+    caption = 16 * ((order % 32) // 8) + 8 * (order // 32) + order % 8
+    r.pair_v[...] = jnp.sum(
+        jnp.where(iota((64, 64), 1) == caption, column.astype(F32), 0.0), axis=1, keepdims=True
+    )
+
+    rows_i = iota((128, 128), 0)
+    lanes_i = iota((128, 128), 1)
+    r.causal[...] = jnp.where(
+        (rows_i // 16 == lanes_i // 16) & (lanes_i <= rows_i), 1.0, 0.0
+    ).astype(F32)
+
+    def emb_copy(index, dev, pick):
+        ref = pick()
+        return rcopy(ref, ref, r.ems.at[max(index - 2, 0)], r.emr.at[index], dev)
+
+    def image_phase(iq, io, iu, idn, low, high, qt, pn, x0, lows):
+        copies = [
+            pltpu.make_async_copy(r.fqkv_h, iq, r.loc.at[1]),
+            pltpu.make_async_copy(r.high_h, high, r.loc.at[2]),
+            pltpu.make_async_copy(r.low_h, low, r.loc.at[3]),
+            pltpu.make_async_copy(r.fout_h, io, r.loc.at[4]),
+            pltpu.make_async_copy(r.fup_h, iu, r.loc.at[5]),
+            pltpu.make_async_copy(r.fdown_h, idn, r.loc.at[6]),
+        ]
+        for copy in copies:
+            copy.start()
+        copies[1].wait()
+        copies[2].wait()
+        g1 = r.fg_v[0:1, :]
+        g2 = r.fg_v[1:2, :]
+        x0[0:2, :] = low[0].astype(F32)
+        for n in range(50):
+            lows[2 * n : 2 * n + 2, :] = low[n].astype(F32)
+        for b in range(14):
+            x0[b + 2 : b + 3, :] = high[b, 0:1, :].astype(F32)
+        centre, inv = stats(x0[...])
+        first = (centre * inv * g1).astype(BF)
+        copies[0].wait()
+        query = nn(first, iq[0]).astype(BF).astype(F32) * 0.125
+        head = iota((16, 768), 1) // 64 == iota((16, 768), 0)
+        spread = jnp.concatenate(
+            [jnp.where(head, query[b : b + 1, :], 0.0).astype(BF) for b in range(16)], axis=0
+        )
+        qt[...] = nt(spread, iq[1]).astype(BF)
+
+        def attend(rows, slot, keep=None):
+            centre, inv = stats(rows)
+            normed = (centre * inv * g1).astype(BF)
+            at = pl.ds(pl.multiple_of(slot * 16, 16), 16)
+            scores = nt(qt[at, :], normed)
+            if keep is not None:
+                scores = jnp.where(keep, scores, -1e30)
+            e = jnp.exp(scores - jnp.max(scores, axis=-1, keepdims=True))
+            soft = (e / jnp.sum(e, axis=-1, keepdims=True)).astype(BF)
+            pn[at, :] = nn(soft, normed).astype(BF)
+
+        for b in range(2):
+            attend(lows[...], b, iota((16, 100), 1) % 2 == b)
+
+        def some(b, carry):
+            attend(high[b].astype(F32), b + 2)
+            return carry
+
+        ag_step(0, 1, 0)
+        lax.fori_loop(0, 2, some, 0)
+        ag_step(0, 1, 1)
+        lax.fori_loop(2, 5, some, 0)
+        ag_step(0, 2, 0)
+        lax.fori_loop(5, 7, some, 0)
+        ag_step(0, 2, 1)
+        lax.fori_loop(7, 10, some, 0)
+        ag_step(0, 3, 0)
+        ag_own(1, 0)
+        text_norm()
+        ag_step(0, 3, 1)
+        ag_own(1, 1)
+        lax.fori_loop(10, 13, some, 0)
+        ag_done(0)
+        attention_forward(0)
+        ag_step(1, 1, 0)
+        attention_forward(1)
+        ar_mid(0, 0, r.cr1, r.xr1)
+        ag_step(1, 1, 1)
+        attention_forward(2)
+        ar_mid(0, 1, r.cr1, r.xr1)
+        ag_step(1, 2, 0)
+        attention_forward(3)
+        ar_mid(0, 2, r.cr1, r.xr1)
+        ag_step(1, 2, 1)
+        lax.fori_loop(13, 14, some, 0)
+        ar_mid(0, 3, r.cr1, r.xr1)
+        values = nn(pn[...], iq[2])
+        head_all = iota((256, 768), 1) // 64 == iota((256, 768), 0) % 16
+        picked = jnp.where(head_all, values, 0.0).astype(BF)
+        chooser = jnp.where(iota((16, 256), 1) // 16 == iota((16, 256), 0), 1.0, 0.0).astype(BF)
+        context = nn(chooser, picked).astype(BF)
+        copies[3].wait()
+        after = x0[...] + nn(context, io[...])
+        centre, inv = stats(after)
+        second = (centre * inv * g2).astype(BF)
+        ag_step(1, 3, 0)
+        ag_own(2, 0)
+        copies[4].wait()
+        copies[5].wait()
+        leading = after
+        for t in range(4):
+            cols = slice(768 * t, 768 * (t + 1))
+            hidden = gelu_only(nn(second, iu[:, cols])).astype(BF)
+            leading = leading + nn(hidden, idn[cols, :])
+        norm = lax.rsqrt(jnp.sum(leading * leading, axis=1, keepdims=True) + 1e-06)
+        r.emb[mp, y, z] = (leading * norm).astype(BF)
+        for k in (1, 2, 3):
+            go(partial(emb_copy, k - 1, zpeer[k], lambda: r.emb.at[mp, y, z]), False)
+
+    def emb_y():
+        for k in (1, 2, 3):
+            emb_copy(k - 1, zpeer[k], lambda: r.emb.at[mp, y, (z - k + 4) % 4]).wait_recv()
+        go(lambda: emb_copy(3, ynb, lambda: r.emb.at[mp, y]))
+
+    def emb_x():
+        emb_copy(3, ynb, lambda: r.emb.at[mp, 1 - y]).wait_recv()
+        go(lambda: emb_copy(4, xnb, lambda: r.emb.at[mp]))
+        go(lambda: emb_copy(5, sib, lambda: r.emb.at[mp]))
+
+    def emb_c():
+        emb_copy(4, xnb, lambda: r.emb.at[(1 - x) * 2 + c]).wait_recv()
+        go(lambda: emb_copy(6, sib, lambda: r.emb.at[(1 - x) * 2 + c]))
+
+    def emb_done():
+        emb_copy(5, sib, lambda: r.emb.at[x * 2 + 1 - c]).wait_recv()
+        emb_copy(6, sib, lambda: r.emb.at[(1 - x) * 2 + 1 - c]).wait_recv()
+
+    def text_norm():
+        for k in range(1, 8):
+            norm_copy(k, lambda: (dp - k + 8) % 8).wait_recv()
+        place_r = iota((1024, 768), 0)
+        place = jnp.where(
+            (iota((1024, 768), 1) == (place_r // 128) * 96 + place_r % 128) & (place_r % 128 < 96), 1.0, 0.0
+        ).astype(BF)
+        r.normp[...] = nn(jnp.concatenate([r.nslot[i] for i in range(8)], axis=1), place)
+        cap_copy.wait()
+        for k in range(CHUNKS):
+            rows = slice(256 * k, 256 * (k + 1))
+            values = r.cap[rows, :].astype(F32)
+            mu = jnp.mean(values, axis=-1, keepdims=True)
+            centre = values - mu
+            inv = lax.rsqrt(jnp.mean(centre * centre, axis=-1, keepdims=True) + 1e-05)
+            r.mu[rows, :] = mu
+            r.rs[rows, :] = inv
+            r.n1[rows, :] = (centre * inv * r.normp[0:1, :] + r.normp[1:2, :]).astype(BF)
+
+    lane = iota((1, 128), 1)
+    lo = jnp.where(lane < 64, 1.0, 0.0).astype(BF)
+    hi = jnp.where(lane < 64, 0.0, 1.0).astype(BF)
+    is_lo = iota((128, 128), 1) < 64
+
+    def attention_forward(k):
+        rows = slice(256 * k, 256 * (k + 1))
+        r.proj[rows, :] = nn(r.n1[rows, :], w[0, :, 0:640]).astype(BF)
+        for b in (2 * k, 2 * k + 1):
+            at = slice(128 * b, 128 * (b + 1))
+            t = [r.proj[at, 128 * i : 128 * (i + 1)] for i in range(5)]
+            keep = (r.causal[...] * r.alive[b : b + 1, :]) > 0.5
+            probs = []
+            for h, (left, right) in enumerate(((t[0] * lo, t[1]), (t[0] * hi, t[1]), (t[3] * lo, t[4]))):
+                s = jnp.where(keep, nt(left, right) * 0.125, -1e30)
+                e = jnp.exp(s - jnp.max(s, axis=-1, keepdims=True))
+                p = e * (1.0 / jnp.sum(e, axis=-1, keepdims=True))
+                r.p[b, h] = p
+                probs.append(p.astype(BF))
+            pair = nn(
+                jnp.concatenate([probs[0], probs[1]], axis=1),
+                jnp.concatenate([t[2] * lo, t[2] * hi], axis=0),
+            )
+            r.o[at, 0:128] = nn(probs[2], t[3] * hi).astype(BF)
+            r.o[at, 128:256] = pair.astype(BF)
+        r.part[rows, :] = nt(r.o[rows, :], w[0, :, 512:768])
+        ar_start(0, k, r.cr1)
+
+    def own_alive(k):
+        row = r.alive[pl.ds(2 * k + c, 1), :]
+        return jnp.where(iota((8, 128), 1) // 16 == iota((8, 128), 0), row, 0.0)
+
+    def chunk_alive(k):
+        row = jnp.concatenate([r.alive[2 * k : 2 * k + 1, :], r.alive[2 * k + 1 : 2 * k + 2, :]], axis=1)
+        return jnp.where(iota((16, 256), 1) // 16 == iota((16, 256), 0), row, 0.0).astype(BF)
+
+    def second_norm(k):
+        a = r.cap[own_rows(k), :].astype(F32) + ar_end(0, k, r.xr1)
+        r.a[k] = a
+        centre, inv = stats(a)
+        r.n2[own_rows(k), :] = (centre * inv * r.normp[2:3, :] + r.normp[3:4, :]).astype(BF)
+        share(0, k, r.n2)
+        alive = own_alive(k)
+        at = slice(8 * k, 8 * (k + 1))
+        r.asum[at, :] = jnp.dot(alive, a, precision=HIGHEST, preferred_element_type=F32)
+        r.cnt[at, :] = jnp.broadcast_to(jnp.sum(alive, axis=1, keepdims=True), (8, 128))
+
+    def mlp_up(k):
+        rows = slice(256 * k, 256 * (k + 1))
+        share_wait(0, k, r.n2)
+        value, slope = gelu_pair(nn(r.n2[rows, :], w[1]))
+        r.gp[rows, :] = slope
+        sums = nn(chunk_alive(k), value.astype(BF))
+        r.hs[0, 8 * k : 8 * (k + 1), :] = sums[0:8]
+        r.hs[1, 8 * k : 8 * (k + 1), :] = sums[8:16]
+
+    pl.run_scoped(
+        image_phase,
+        pltpu.VMEM((3, 768, 768), BF),
+        pltpu.VMEM((768, 768), BF),
+        pltpu.VMEM((768, 3072), BF),
+        pltpu.VMEM((3072, 768), BF),
+        pltpu.VMEM((50, 2, 768), BF),
+        pltpu.VMEM((14, 145, 768), BF),
+        pltpu.VMEM((256, 768), BF),
+        pltpu.VMEM((256, 768), BF),
+        pltpu.VMEM((16, 768), F32),
+        pltpu.VMEM((100, 768), F32),
+    )
+
+    ag_step(1, 3, 1)
+    ag_own(2, 1)
+    second_norm(0)
+    ag_done(1)
+    ag_step(2, 1, 0)
+    mlp_up(0)
+    second_norm(1)
+    ag_step(2, 1, 1)
+    emb_y()
+    mlp_up(1)
+    ag_step(2, 2, 0)
+    second_norm(2)
+    ag_step(2, 2, 1)
+    emb_x()
+    mlp_up(2)
+    ag_step(2, 3, 0)
+    second_norm(3)
+    ag_step(2, 3, 1)
+    emb_c()
+    mlp_up(3)
+
+    hsum = r.hs[...].reshape(64, 768)
+    high_part = hsum.astype(BF)
+    r.hl[0:64, :] = high_part
+    r.hl[64:128, :] = (hsum - high_part.astype(F32)).astype(BF)
+    ag_done(2)
+    both = nt(r.hl[...], w[2])
+    r.pp[...] = (both[0:64] + both[64:128]).reshape(2, 32, 768)
+    first_copy = go(lambda: rcopy(r.pp.at[1 - c], r.pcr, r.pos.at[0], r.por.at[0], sib))
+    emb_done()
+    first_copy.wait_recv()
+    r.pxs[...] = r.pp[c] + r.pcr[...]
+    second_copy = go(lambda: rcopy(r.pxs, r.pxr, r.pos.at[1], r.por.at[1], xnb))
+    count = r.cnt[:, 0:1]
+    second_copy.wait_recv()
+    pooled = (r.asum[...] + (r.pxs[...] + r.pxr[...])) / count
+    inverse = lax.rsqrt(jnp.sum(pooled * pooled, axis=1, keepdims=True) + 1e-06)
+    unit = pooled * inverse
+    images = r.emb[...].reshape(total_caps, 768)
+    logits = logit_scale * nt(unit.astype(BF), images)
+    top = jnp.max(logits, axis=1, keepdims=True)
+    row_lse = top + jnp.log(jnp.sum(jnp.exp(logits - top), axis=1, keepdims=True))
+    match = iota((32, total_caps), 1).astype(F32) == r.pair_v[pl.ds(pl.multiple_of(32 * c, 32), 32), :]
+    dlogits = (jnp.exp(logits - row_lse) - jnp.where(match, 1.0, 0.0)) / total_caps
+    dunit = nn((logit_scale * dlogits).astype(BF), images)
+    dpooled = inverse * (dunit - unit * jnp.sum(unit * dunit, axis=1, keepdims=True))
+    dpc = dpooled / count
+    r.dpc[...] = dpc
+    r.dy[c] = dpc.astype(BF)
+
+    def dy_copy(core):
+        ref = r.dy.at[core]
+        return rcopy(ref, ref, r.pos.at[2], r.por.at[2], sib)
+
+    go(lambda: dy_copy(c))
+
+    def backward(du, dpack, g, packed, raw):
+        moments = ((r.fiq_h, r.fio_h, r.fiu_h, r.fid_h), (r.seq_h, r.seo_h, r.seu_h, r.sed_h))
+        raw_copies = []
+        for m in range(2):
+            for n in range(4):
+                copy = pltpu.make_async_copy(moments[m][n], raw[4 * m + n], r.loc.at[7 + 4 * m + n])
+                copy.start()
+                raw_copies.append(copy)
+
+        def mlp_backward(k):
+            rows = slice(256 * k, 256 * (k + 1))
+            dh = jnp.concatenate(
+                [r.dh[0, 8 * k : 8 * (k + 1), :], r.dh[1, 8 * k : 8 * (k + 1), :]], axis=0
+            )
+            dh_high = dh.astype(BF)
+            dh_low = (dh - dh_high.astype(F32)).astype(BF)
+            alive = chunk_alive(k)
+            spread = tn(jnp.concatenate([alive, alive], axis=0), jnp.concatenate([dh_high, dh_low], axis=0))
+            value = (r.gp[rows, :] * spread).astype(BF)
+            du[rows, :] = value
+            r.part[rows, :] = nt(value, w[1])
+            ar_start(1, k, r.cr2)
+
+        def rs_copy(kind, way, index):
+            return rcopy(
+                r.rss.at[kind, way, index], r.rsr.at[kind, way, index],
+                r.rsa.at[kind], r.rsb.at[kind, way, index], ways[way],
+            )
+
+        def rs_index(step, half):
+            return 0 if step == 0 else 2 * step - 1 + half
+
+        def rs_send(kind, way, step, half, add):
+            k = 4 - step if way == 0 else step - 4
+            value = g[kind, piece(k, half), :]
+            if add:
+                before = rs_index(step - 1, half)
+                rs_copy(kind, way, before).wait_recv()
+                value = value + r.rsr[kind, way, before].astype(F32)
+            index = rs_index(step, half)
+            r.rss[kind, way, index] = value.astype(BF)
+            go(partial(rs_copy, kind, way, index), False)
+
+        def rs_start(kind):
+            for way in (0, 1):
+                rs_send(kind, way, 0, way, False)
+            for way in (0, 1):
+                rs_send(kind, way, 1, 1 - way, False)
+
+        def rs_step(kind, step, early):
+            for way in (0, 1):
+                rs_send(kind, way, step, 1 - way if early else way, True)
+
+        def rs_end(kind):
+            for half in (0, 1):
+                index = rs_index(3, half)
+                for way in (0, 1):
+                    rs_copy(kind, way, index).wait_recv()
+                r.gsh[kind, 48 * half : 48 * half + 48, :] = g[kind, piece(0, half), :] + (
+                    r.rsr[kind, 0, index].astype(F32) + r.rsr[kind, 1, index].astype(F32)
+                )
+
+        def second_backward(k, dgain, dshift):
+            dn = ar_end(1, k, r.xr2)
+            centre, inv = stats(r.a[k])
+            hat = centre * inv
+            dhat = dn * r.normp[2:3, :]
+            dln = inv * (
+                dhat - jnp.mean(dhat, axis=-1, keepdims=True)
+                - hat * jnp.mean(dhat * hat, axis=-1, keepdims=True)
+            )
+            dout = lax.dot_general(
+                own_alive(k), r.dpc[8 * k : 8 * (k + 1), :], (((0,), (0,)), ((), ())),
+                precision=HIGHEST, preferred_element_type=F32,
+            )
+            da = dout + dln
+            r.a[k] = da
+            r.dz[own_rows(k), :] = da.astype(BF)
+            share(1, k, r.dz)
+            return (
+                dgain + jnp.sum(dn * hat, axis=0, keepdims=True),
+                dshift + jnp.sum(dn, axis=0, keepdims=True),
+            )
+
+        def attention_backward(k, dgain, dshift):
+            rows = slice(256 * k, 256 * (k + 1))
+            share_wait(1, k, r.dz)
+            do_all = nn(r.dz[rows, :], w[0, :, 512:768]).astype(BF)
+            for i, b in enumerate((2 * k, 2 * k + 1)):
+                at = slice(128 * b, 128 * (b + 1))
+                t = [r.proj[at, 128 * j : 128 * (j + 1)] for j in range(5)]
+                do2 = do_all[128 * i : 128 * (i + 1), 0:128] * hi
+                do01 = do_all[128 * i : 128 * (i + 1), 128:256]
+                ds, ps = [], []
+                for h, (left, right) in enumerate(((do01 * lo, t[2]), (do01 * hi, t[2]), (do2, t[3]))):
+                    dw = nt(left, right)
+                    p = r.p[b, h]
+                    ps.append(p.astype(BF))
+                    ds.append((p * (dw - jnp.sum(p * dw, axis=-1, keepdims=True))).astype(BF))
+                dq = nn(
+                    jnp.concatenate([ds[0], ds[1]], axis=1),
+                    jnp.concatenate([t[1] * lo, t[1] * hi], axis=0),
+                )
+                dk = tn(
+                    jnp.concatenate([ds[0], ds[1]], axis=0),
+                    jnp.concatenate([t[0] * lo, t[0] * hi], axis=0),
+                )
+                dv = tn(
+                    jnp.concatenate([ps[0], ps[1]], axis=0),
+                    jnp.concatenate([do01 * lo, do01 * hi], axis=0),
+                )
+                dq2 = nn(ds[2], t[4] * lo)
+                dk2 = tn(ds[2], t[3] * lo)
+                dv2 = tn(ps[2], do2)
+                dpack[at, 0:128] = (dq * 0.125).astype(BF)
+                dpack[at, 128:256] = (dk * 0.125).astype(BF)
+                dpack[at, 256:384] = dv.astype(BF)
+                dpack[at, 384:512] = (dq2 * 0.125 + dv2).astype(BF)
+                dpack[at, 512:640] = (dk2 * 0.125).astype(BF)
+            part = nt(dpack[rows, :], w[0, :, 0:640])
+            r.part[rows, :] = part
+            ar_start(2, k, r.cr1)
+            inner = tn(r.n1[rows, :], dpack[rows, :])
+            outer = tn(r.dz[rows, :], r.o[rows, :])
+            if k == 0:
+                g[0, :, 0:512] = inner[:, 0:512]
+                g[0, :, 512:640] = inner[:, 512:640] + outer[:, 0:128]
+                g[0, :, 640:768] = outer[:, 128:256]
+            else:
+                g[0, :, 0:512] += inner[:, 0:512]
+                g[0, :, 512:640] += inner[:, 512:640] + outer[:, 0:128]
+                g[0, :, 640:768] += outer[:, 128:256]
+            hat = (r.cap[rows, :].astype(F32) - r.mu[rows, :]) * r.rs[rows, :]
+            return (
+                dgain + jnp.sum(part * hat, axis=0, keepdims=True),
+                dshift + jnp.sum(part, axis=0, keepdims=True),
+            )
+
+        dy_copy(1 - c).wait_recv()
+        dy = r.dy[...].reshape(64, 768)
+        g[2] = tn(jnp.concatenate([dy, dy], axis=0), r.hl[...])
+        rs_start(2)
+        r.dh[...] = nn(dy, w[2]).reshape(2, 32, 768)
+
+        mlp_backward(0)
+        mlp_backward(1)
+        ar_mid(1, 0, r.cr2, r.xr2)
+        rs_step(2, 1, False)
+        mlp_backward(2)
+        ar_mid(1, 1, r.cr2, r.xr2)
+        rs_step(2, 2, True)
+        mlp_backward(3)
+        ar_mid(1, 2, r.cr2, r.xr2)
+        rs_step(2, 2, False)
+        ar_mid(1, 3, r.cr2, r.xr2)
+        g[1] = tn(r.n2[...], du[...])
+        rs_start(1)
+        rs_step(2, 3, True)
+        zero = jnp.zeros((1, 768), F32)
+        dg2, db2, dg1, db1 = zero, zero, zero, zero
+        dg2, db2 = second_backward(0, dg2, db2)
+        rs_step(2, 3, False)
+        dg1, db1 = attention_backward(0, dg1, db1)
+        dg2, db2 = second_backward(1, dg2, db2)
+        ar_mid(2, 0, r.cr1, r.xr1)
+        rs_step(1, 1, False)
+        rs_end(2)
+        dg1, db1 = attention_backward(1, dg1, db1)
+        rs_step(1, 2, True)
+        dg2, db2 = second_backward(2, dg2, db2)
+        ar_mid(2, 1, r.cr1, r.xr1)
+        rs_step(1, 2, False)
+        dg1, db1 = attention_backward(2, dg1, db1)
+        rs_step(1, 3, True)
+        dg2, db2 = second_backward(3, dg2, db2)
+        ar_mid(2, 2, r.cr1, r.xr1)
+        rs_step(1, 3, False)
+        dg1, db1 = attention_backward(3, dg1, db1)
+        rs_start(0)
+        ar_mid(2, 3, r.cr1, r.xr1)
+
+        def gn_core():
+            return rcopy(r.gns, r.gnr, r.gss.at[0], r.gsr.at[7], sib)
+
+        def gn_slice(k):
+            return rcopy(r.gsl.at[(dp + k) % 8], r.gslr.at[k - 1], r.gss.at[1], r.gsr.at[k - 1], dpeer[k])
+
+        def gn_x():
+            return rcopy(r.gslr.at[7], r.gslr.at[8], r.gss.at[2], r.gsr.at[8], xnb)
+
+        r.gns[...] = jnp.concatenate(
+            [dg1, db1, 0.5 * dg2, 0.5 * db2, jnp.zeros((4, 768), F32)], axis=0
+        )
+        go(gn_core)
+
+        def out_copy(k, rows):
+            return rcopy(
+                r.a.at[k], r.ig_o.at[rows(k)], r.shs.at[2], r.shr.at[2, k], sib
+            )
+
+        def finish_rows(k):
+            dn = ar_end(2, k, r.xr1)
+            hat = (r.cap[own_rows(k), :].astype(F32) - r.mu[own_rows(k), :]) * r.rs[own_rows(k), :]
+            dhat = dn * r.normp[0:1, :]
+            dln = r.rs[own_rows(k), :] * (
+                dhat - jnp.mean(dhat, axis=-1, keepdims=True)
+                - hat * jnp.mean(dhat * hat, axis=-1, keepdims=True)
+            )
+            r.a[k] = r.a[k] + dln
+            local = pltpu.make_async_copy(r.a.at[k], r.ig_o.at[own_rows(k)], r.outs.at[k])
+            local.start()
+            go(lambda: out_copy(k, own_rows), False)
+            return local
+
+        for t, tile in enumerate(tiles):
+            packed[0, 0, :, 128 * t : 128 * (t + 1)] = tile
+        packed[0, 1] = r.up_v[...]
+        packed[0, 2] = r.down_v[...]
+        for copy in raw_copies:
+            copy.wait()
+        for m in range(2):
+            for t, tile in enumerate(pack_attn(raw[4 * m], raw[4 * m + 1])):
+                packed[1 + m, 0, :, 128 * t : 128 * (t + 1)] = tile
+            packed[1 + m, 1] = raw[4 * m + 2][...]
+            packed[1 + m, 2] = raw[4 * m + 3][...]
+
+        gn_core().wait_recv()
+        gn_pad = jnp.concatenate([r.gns[...] + r.gnr[...], jnp.zeros((8, 128), F32)], axis=1)
+        for i in range(8):
+            r.gsl[i] = gn_pad[:, 96 * i : 96 * i + 128]
+        for k in range(1, 8):
+            go(partial(gn_slice, k), False)
+        rs_step(0, 1, False)
+        locals_out = [finish_rows(0)]
+        rs_step(0, 2, True)
+        locals_out.append(finish_rows(1))
+        rs_end(1)
+        rs_step(0, 2, False)
+        gn_mine = r.gsl[dp]
+        for k in range(1, 8):
+            gn_slice(k).wait_recv()
+            gn_mine = gn_mine + r.gslr[k - 1]
+        r.gslr[7] = gn_mine
+        go(gn_x)
+        locals_out.append(finish_rows(2))
+        rs_step(0, 3, True)
+        locals_out.append(finish_rows(3))
+        rs_step(0, 3, False)
+        gn_x().wait_recv()
+        gn_mine = jnp.where(iota((8, 128), 1) < 96, gn_mine + r.gslr[8], 0.0)
+        r.gn[...] = gn_mine
+        finals = [pltpu.make_async_copy(r.gn, r.gn_o, r.fin.at[3])]
+        finals[0].start()
+
+        sel_lane = iota((8, 128), 1)
+        sel_row = iota((8, 128), 0)
+        squares = jnp.zeros((8, 128), F32)
+
+        def put(acc, row, index, value):
+            return acc + jnp.where((sel_row == row) & (sel_lane == index), value, 0.0)
+
+        quarter = 0.25
+        zeros4 = jnp.zeros((4, 96), F32)
+        gn4 = gn_mine[0:4, 0:96]
+        norm_update, _, _ = lamb_update(r.norms_v[...], gn4, r.fin_v[...], r.sen_v[...])
+        for row, value in ((0, r.norms_v[...]), (1, norm_update)):
+            line = quarter * jnp.sum(value * value, axis=1, keepdims=True)
+            for n in range(4):
+                squares = put(squares, row, 6 + n, line[n : n + 1, :])
+        lane_all = iota((1, 768), 1)
+        third = (lane_all // 64) % 12
+        owner = jnp.where(
+            lane_all < 384, lane_all // 128,
+            jnp.where(
+                lane_all < 512, jnp.where(lane_all < 448, 0, 2),
+                jnp.where(lane_all < 576, 1, 3),
+            ),
+        )
+        for kind in (2, 1, 0):
+            if kind == 0:
+                rs_end(0)
+            final = pltpu.make_async_copy(r.gsh.at[kind], r.gsh_o.at[kind], r.fin.at[kind])
+            final.start()
+            finals.append(final)
+            update, _, _ = lamb_update(packed[0, kind], r.gsh[kind], packed[1, kind], packed[2, kind])
+            for row, value in ((0, packed[0, kind]), (1, update)):
+                line = jnp.sum(value * value, axis=0, keepdims=True)
+                if kind == 0:
+                    for n in range(4):
+                        part = jnp.sum(jnp.where(owner == n, line, 0.0), axis=1, keepdims=True)
+                        squares = put(squares, row, n, part)
+                else:
+                    squares = put(squares, row, 3 + kind, jnp.sum(line, axis=1, keepdims=True))
+
+        sqd, sqm = r.sqd, r.sqm
+
+        def sq_copy(buffer, slot, index, dev):
+            ref = buffer.at[slot()]
+            return rcopy(ref, ref, r.sqs.at[index // 7], r.sqr.at[index], dev)
+
+        sqd[dp] = squares
+        for k in range(1, 8):
+            go(partial(sq_copy, sqd, lambda: dp, k - 1, dpeer[k]), False)
+        for k in range(1, 8):
+            sq_copy(sqd, lambda: (dp - k + 8) % 8, k - 1, dpeer[k]).wait_recv()
+        total = sqd[0]
+        for i in range(1, 8):
+            total = total + sqd[i]
+        sqm[mp] = total
+        others = ((sib, x * 2 + 1 - c), (xnb, (1 - x) * 2 + c), (diag, (1 - x) * 2 + 1 - c))
+        for n, (dev, _) in enumerate(others):
+            go(partial(sq_copy, sqm, lambda: mp, 7 + n, dev), False)
+        for n, (dev, source) in enumerate(others):
+            sq_copy(sqm, lambda: source, 7 + n, dev).wait_recv()
+        r.tot[...] = (sqm[0] + sqm[1]) + (sqm[2] + sqm[3])
+        final = pltpu.make_async_copy(r.tot, r.tot_o, r.fin.at[4])
+        final.start()
+        finals.append(final)
+        for local in locals_out + finals:
+            local.wait()
+        for k in range(CHUNKS):
+            out_copy(k, sib_rows).wait_recv()
+
+    pl.run_scoped(
+        backward,
+        pltpu.VMEM((1024, 768), BF),
+        pltpu.VMEM((1024, 640), BF),
+        pltpu.VMEM((3, 768, 768), F32),
+        pltpu.VMEM((3, 3, 96, 768), F32),
+        [
+            pltpu.VMEM(shape, F32)
+            for _ in range(2)
+            for shape in ((3, 96, 192), (192, 96), (96, 768), (96, 768))
+        ],
+    )
+    for make in sends:
+        make().wait_send()
+
+    def all_sent(ref, sem):
+        rcopy(ref, ref, sem, sem, sib).wait_send()
+
+    all_sent(r.nslot.at[pl.ds(0, 7)], r.nsem.at[7])
+    for kind in range(3):
+        all_sent(w.at[kind, pl.ds(0, 672)], r.ags.at[kind])
+        all_sent(r.rss.at[kind], r.rsa.at[kind])
+    all_sent(r.n2.at[pl.ds(0, 512)], r.shs.at[0])
+    all_sent(r.dz.at[pl.ds(0, 512)], r.shs.at[1])
+    all_sent(r.a, r.shs.at[2])
+    all_sent(r.emb.at[0, 0, pl.ds(0, 3)], r.ems.at[0])
+    all_sent(r.gslr.at[pl.ds(0, 7)], r.gss.at[1])
+    all_sent(r.sqd.at[pl.ds(0, 7)], r.sqs.at[0])
+    all_sent(r.sqm.at[pl.ds(0, 3)], r.sqs.at[1])
+
+
+def lamb_kernel(*refs):
+    sources, targets = refs[0:19], refs[19:46]
+    buffers, results = refs[46:64], refs[64:90]
+    rows, in_sem, out_sem = refs[90:93]
+    pieces = []
+    for n in range(4):
+        at = pl.ds(256 * n, 256)
+        pieces.append(
+            (
+                pltpu.make_async_copy(sources[18].at[at], rows.at[at], in_sem.at[18 + n]),
+                pltpu.make_async_copy(rows.at[at], targets[26].at[at], out_sem.at[26 + n]),
+            )
+        )
+    loads = [pltpu.make_async_copy(sources[n], buffers[n], in_sem.at[n]) for n in range(18)]
+    for copy in loads:
+        copy.start()
+    for load, _ in pieces:
+        load.start()
+    stores = []
+    (gsh, gn, tot, w_qkv, w_out, w_up, w_down, w_norms, m_qkv, m_out, m_up, m_down, m_norms,
+     v_qkv, v_out, v_up, v_down, v_norms) = buffers
+    grads, news, copies, means, squares = (results[5 * i : 5 * i + 5] for i in range(5))
+
+    def store(n):
+        copy = pltpu.make_async_copy(results[n], targets[n], out_sem.at[n])
+        copy.start()
+        stores.append(copy)
+
+    def ready(*which):
+        for n in which:
+            loads[n].wait()
+
+    def rows_through(n):
+        pieces[n][0].wait()
+        pieces[n][1].start()
+        stores.append(pieces[n][1])
+
+    ready(0, 1, 2, 5, 10, 15)
+    roots = jnp.sqrt(tot[0:2, :])
+    results[25][...] = roots[:, 0:10]
+    store(25)
+    ratio = learning_rate * (roots[0:1, :] / roots[1:2, :])
+
+    def one(index, at, scale, grad, weight, first, second):
+        update, mean_new, square_new = lamb_update(weight, grad, first, second)
+        fresh = weight - scale * update
+        for group, value in zip(
+            (grads, news, copies, means, squares), (grad, fresh, fresh.astype(BF), mean_new, square_new)
+        ):
+            group[index][at] = value
+
+    def send(index):
+        for group in range(5):
+            store(5 * group + index)
+
+    one(2, Ellipsis, ratio[:, 4:5], gsh[1], w_up[...], m_up[...], v_up[...])
+    send(2)
+    ready(6, 11, 16)
+    one(3, Ellipsis, ratio[:, 5:6], gsh[2], w_down[...], m_down[...], v_down[...])
+    send(3)
+    ready(3, 8, 13)
+    attn = gsh[0]
+    third = attn[:, 384:512]
+    fourth = attn[:, 512:640]
+    parts = (
+        jnp.concatenate([attn[:, 0:128], third[:, 0:64]], axis=1),
+        jnp.concatenate([attn[:, 128:256], fourth[:, 0:64]], axis=1),
+        jnp.concatenate([attn[:, 256:384], third[:, 64:128]], axis=1),
+    )
+    for n in range(3):
+        one(0, n, ratio[:, n : n + 1], parts[n], w_qkv[n], m_qkv[n], v_qkv[n])
+    send(0)
+    rows_through(0)
+    rows_through(1)
+    ready(4, 9, 14)
+    out_grad = jnp.concatenate([attn[:, 640:768], fourth[:, 64:128]], axis=1).T
+    one(1, Ellipsis, ratio[:, 3:4], out_grad, w_out[...], m_out[...], v_out[...])
+    send(1)
+    rows_through(2)
+    rows_through(3)
+    ready(7, 12, 17)
+    for n in range(4):
+        at = (slice(n, n + 1), slice(None))
+        one(4, at, ratio[:, 6 + n : 7 + n], gn[n : n + 1, 0:96], w_norms[at], m_norms[at], v_norms[at])
+    send(4)
+    for copy in stores:
+        copy.wait()
+
+
+def fused_shards(
+    captions, token_ids, pairing, low_images, high_images, frozen_qkv, frozen_out, frozen_up,
+    frozen_down, frozen_gains, *state
+):
+    masters, firsts, seconds = state[0:5], state[5:10], state[10:15]
+    cap_rows, seq_rows, width_all = captions.shape
+    rows = cap_rows * seq_rows
+    total_caps = cap_rows * lax.axis_size("dp")
+    swapped = [
+        tuple(a.T if n == 3 else a for n, a in enumerate(group)) for group in (masters, firsts, seconds)
+    ]
+    table = scratch_table()
+    hbm = pl.BlockSpec(memory_space=pltpu.HBM)
+    ins = dict(
+        cap_h=captions.reshape(rows, width_all), tok_h=token_ids.T, pair_h=pairing.reshape(1, cap_rows),
+        low_h=low_images.transpose(1, 0, 2), high_h=high_images, fqkv_h=frozen_qkv, fout_h=frozen_out,
+        fup_h=frozen_up, fdown_h=frozen_down, fg_h=frozen_gains,
+    )
+    for key, group in zip(("m", "fi", "se"), swapped):
+        ins.update(zip((key + part for part in ("q_h", "o_h", "u_h", "d_h", "n_h")), group))
+    results = dict(
+        ig_o=jax.ShapeDtypeStruct((rows, width_all), F32),
+        gsh_o=jax.ShapeDtypeStruct((3, 96, width_all), F32),
+        gn_o=jax.ShapeDtypeStruct((8, 128), F32),
+        tot_o=jax.ShapeDtypeStruct((8, 128), F32),
+    )
+    names = tuple(ins) + tuple(results) + tuple(table)
+    grad_in, gsh, gn, tot = pl.pallas_call(
+        partial(step_kernel, names, total_caps),
+        out_shape=tuple(results.values()),
+        in_specs=[hbm] * len(ins),
+        out_specs=tuple([hbm] * len(results)),
+        scratch_shapes=list(table.values()),
+        compiler_params=pltpu.CompilerParams(
+            collective_id=0, has_side_effects=True, vmem_limit_bytes=62 * 1024 * 1024
+        ),
+    )(*ins.values())
+    operands = (gsh, gn, tot, *swapped[0], *swapped[1], *swapped[2])
+    shapes = [m.shape for m in swapped[0]]
+    made = [jax.ShapeDtypeStruct(shape, kind) for kind in (F32, F32, BF, F32, F32) for shape in shapes]
+    made.append(jax.ShapeDtypeStruct((2, 10), F32))
+    outs = pl.pallas_call(
+        lamb_kernel,
+        out_shape=tuple(made) + (jax.ShapeDtypeStruct(grad_in.shape, F32),),
+        in_specs=[hbm] * 19,
+        out_specs=tuple([hbm] * 27),
+        scratch_shapes=[pltpu.VMEM(a.shape, a.dtype) for a in operands]
+        + [pltpu.VMEM(m.shape, m.dtype) for m in made]
+        + [
+            pltpu.VMEM(grad_in.shape, F32), pltpu.SemaphoreType.DMA((22,)), pltpu.SemaphoreType.DMA((30,))
+        ],
+        compiler_params=pltpu.CompilerParams(vmem_limit_bytes=62 * 1024 * 1024),
+    )(*operands, grad_in)
+    final = [out.T if n % 5 == 3 and n < 25 else out for n, out in enumerate(outs)]
+    return (final[26].reshape(captions.shape), *final[:26])
+
+
 def solution(mesh):
+    whole = mesh.shape["dp"] == 8 and mesh.shape["mp"] == 4
     return jax.shard_map(
-        shards,
+        fused_shards if whole else shards,
         mesh=mesh,
         in_specs=(
             P("dp", None, None),

time: 888 us -> 125 us (0.14)
  waiting for transfers between devices: 344 us -> 0 us
  blocking collectives: 210 us -> 0 us
  matrix products: 157 us -> 0 us
  Pallas kernels: 0 us -> 124 us
  local copies, waits for them, and re-layouts: 88.1 us -> 0 us
  other arithmetic: 65 us -> 0 us
  between operations: 18.4 us -> 0.88 us
    psum x5 -> x0, waiting for transfers between devices: 344 us -> none  [the longest x1 194 us: shards(): lax.psum((local_grads[0], local_grads[1], local_grads[2], local_grads[3],...]
    dot_general x28 -> x0, matrix products: 133 us -> none  [the longest x2 35.9 us: frozen_embed(): jnp.einsum('blf,fd->bld', hidden, frozen_down, preferred_element_type=jnp...]
    all_gather x4 -> x0, blocking collectives: 132 us -> none  [the longest x1 44.4 us: shards(): images_all = lax.all_gather(local_images, ('dp', 'mp'), axis=0, tiled=True)]
    pallas_call x0 -> x2, Pallas kernels: none -> 124 us  [the longest x1 118 us: fused_shards(): pl.pallas_call(partial(step_kernel, names, total_caps), out_shape=tuple(r...]
    psum x2 -> x0, blocking collectives: 78.5 us -> none  [the longest x1 39.3 us: shards(): lax.psum((local_grads[0], local_grads[1], local_grads[2], local_grads[3],...]
    reduce_sum x27 -> x0, other arithmetic: 40.2 us -> none  [the longest x5 10.2 us: lamb_parts(): weight_sq = jnp.sum(weight * weight, axis=axes)]
    slice x12 -> x0, local copies, waits for them, and re-layouts: 32 us -> none  [the longest x2 9.72 us: frozen_embed(): heads_all[1]]
    unnamed x169 -> x0, local copies, waits for them, and re-layouts: 24.8 us -> none
  transfers between devices with their start and end apart: 7 -> 0, of which waited for: 4 -> 0; matrix products, arithmetic and copies ran while one was open for 19% -> 0% of each run, Pallas kernels for 0% -> 0%
where the time goes in v1:
time: 125 us; the launch traced here: 124 us
  Pallas kernels  124 us (99%)
    pallas_call x1, Pallas kernels, fused_shards(): pl.pallas_call(partial(step_kernel, names, total_caps), out_shape=tuple(r...  118 us
    pallas_call x1, Pallas kernels, fused_shards(): pl.pallas_call(lamb_kernel, out_shape=tuple(made) + (jax.ShapeDtypeStruct...  5.99 us

profile of v1, /device:TPU:0, one launch (start us, length us, event | category | flops | bytes accessed | tf_op | source)
XLA Modules:
  0.0 124.4 jit_solution(9372346680516940073)
XLA Ops:
  0.7 117.5 %shard_map.448 = (f32[1024,768]{1,0:T(8,128)}, f32[3,96,768]{2,1,0:T(8,128)}, f32[8,128]{1,0:T(8,128)}, f32[8,128]{1,0:T(8,128)}) custom-call(bf16[1024,768]{1,0:T(8,128)(2,1)} %bitcast.13, s32[16,64]{1,0:T(8,128)} %bitcast.21, s32[1,64]{1,0:T(1,128)} %bitcast.22, bf16[50,2,768]{2,1,0:T(2,128)(2,1)} %bitcast.20, bf16[14,145,768]{2,1,0:T(8,128)(2,1)} %refs_4_.2, ...), custom_call_target="tpu_custom_call" | custom-call | tf_op jit(solution)/shard_map/pallas_call | solution.py:1347
  118.2 6.0 %shard_map.449 = (f32[3,96,192]{2,1,0:T(8,128)}, f32[192,96]{1,0:T(8,128)}, f32[96,768]{1,0:T(8,128)}, f32[96,768]{1,0:T(8,128)}, f32[4,96]{1,0:T(4,128)}, /*ind...) custom-call(f32[3,96,768]{2,1,0:T(8,128)} %get-tuple-element.58.refs, ...), custom_call_target="tpu_custom_call" | custom-call | tf_op jit(solution)/shard_map/pallas_call | solution.py:1361

commit v2 on v1

--- a/solution.py
+++ b/solution.py
@@ -280,7 +280,6 @@
 MESH = pl.DeviceIdType.MESH
 BF = jnp.bfloat16
 F32 = jnp.float32
-HIGHEST = lax.Precision.HIGHEST
 
 
 def nn(a, b):
@@ -293,6 +292,11 @@
 
 def tn(a, b):
     return lax.dot_general(a, b, (((0,), (0,)), ((), ())), preferred_element_type=F32)
+
+
+def split(values):
+    high = values.astype(BF)
+    return jnp.concatenate([high, (values - high.astype(F32)).astype(BF)], axis=0)
 
 
 def iota(shape, dim):
@@ -378,6 +382,8 @@
         p=vm((8, 3, 128, 128), F32),
         o=vm((1024, 256), BF),
         part=vm((1024, 768), F32),
+        wo=vm((4, 768, 256), BF),
+        oall=vm((4, CHUNKS, 128, 256), BF),
         cs=vm((CHUNKS, 128, 768), BF),
         cr1=vm((CHUNKS, 128, 768), BF),
         cr2=vm((CHUNKS, 128, 768), BF),
@@ -406,8 +412,7 @@
         gnr=vm((8, 768), F32),
         gsl=vm((8, 8, 128), F32),
         gslr=vm((9, 8, 128), F32),
-        sqd=vm((8, 8, 128), F32),
-        sqm=vm((4, 8, 128), F32),
+        sqd=vm((32, 8, 128), F32),
         loc=dma((15,)),
         first=dma((10,)),
         fin=dma((5,)),
@@ -416,6 +421,10 @@
         agr=dma((3, 2, 7)),
         rsa=dma((3,)),
         rsb=dma((3, 2, 7)),
+        wos=dma((3,)),
+        wor=dma((10,)),
+        oas=dma((1,)),
+        oar=dma((3, CHUNKS)),
         arcs=dma((CHUNKS,)),
         arcr=dma((3, CHUNKS)),
         arxs=dma((CHUNKS,)),
@@ -428,8 +437,8 @@
         emr=dma((7,)),
         gss=dma((3,)),
         gsr=dma((9,)),
-        sqs=dma((2,)),
-        sqr=dma((10,)),
+        sqs=dma((1,)),
+        sqr=dma((31,)),
         outs=dma((CHUNKS,)),
     )
 
@@ -452,6 +461,7 @@
 
     ways = ((ring(1), mp), (ring(-1), mp))
     zpeer = {k: (((z + k) % 4) * 2 + y, mp) for k in (1, 2, 3)}
+    everyone = {k: ((dp * 4 + mp + k) % 32 // 4, (mp + k) % 4) for k in range(1, 32)}
     dpeer = {k: ((dp + k) % 8, mp) for k in range(1, 8)}
 
     def rcopy(src, dst, ssem, rsem, dev):
@@ -521,6 +531,47 @@
         ag_copy(kind, 0, 3, 0, -4).wait_recv()
         ag_copy(kind, 1, 3, 1, 4).wait_recv()
 
+    def wo_x(k, source):
+        rows = pl.ds(pl.multiple_of(ring(k) * 96, 16), 96)
+        return rcopy(
+            w.at[0, rows, pl.ds(512, 256)], r.wo.at[source(), rows], r.wos.at[0], r.wor.at[k + 3], xnb
+        )
+
+    def wo_send(*which):
+        for k in which:
+            go(partial(wo_x, k, lambda: mp), False)
+
+    def wo_own(source):
+        return rcopy(w.at[0, :, pl.ds(512, 256)], r.wo.at[source()], r.wos.at[1], r.wor.at[8], sib)
+
+    def wo_across(source):
+        ref = r.wo.at[source()]
+        return rcopy(ref, ref, r.wos.at[2], r.wor.at[9], sib)
+
+    def wo_cores():
+        for k in range(-3, 5):
+            wo_x(k, lambda: (1 - x) * 2 + c).wait_recv()
+        go(lambda: wo_across(lambda: (1 - x) * 2 + c))
+
+    def wo_done():
+        wo_own(lambda: x * 2 + 1 - c).wait_recv()
+        wo_across(lambda: (1 - x) * 2 + 1 - c).wait_recv()
+
+    def o_copy(n, k, source):
+        dev = (sib, xnb, diag)[n]
+        rows = own_rows(k) if n == 1 else sib_rows(k)
+        return rcopy(r.o.at[rows], r.oall.at[source(), k], r.oas.at[0], r.oar.at[n, k], dev)
+
+    def o_send(k):
+        for n in range(3):
+            go(partial(o_copy, n, k, lambda: mp), False)
+        r.oall[mp, k] = r.o[own_rows(k), :]
+
+    def o_wait(k):
+        others = (x * 2 + 1 - c, (1 - x) * 2 + c, (1 - x) * 2 + 1 - c)
+        for n in range(3):
+            o_copy(n, k, lambda: others[n]).wait_recv()
+
     def core_copy(which, k, received):
         return rcopy(r.cs.at[k], received.at[k], r.arcs.at[k], r.arcr.at[which, k], sib)
 
@@ -528,14 +579,14 @@
         return rcopy(r.xs.at[k], received_x.at[k], r.arxs.at[k], r.arxr.at[which, k], xnb)
 
     def ar_start(which, k, received):
-        if which > 0:
+        if which > 1:
             core_copy(which - 1, k, received).wait_send()
         r.cs[k] = r.part[sib_rows(k), :].astype(BF)
         go(lambda: core_copy(which, k, received), which == 2)
 
     def ar_mid(which, k, received, received_x):
         core_copy(which, k, received).wait_recv()
-        if which > 0:
+        if which > 1:
             x_copy(which - 1, k, received_x).wait_send()
         r.xs[k] = (r.part[own_rows(k), :] + received[k].astype(F32)).astype(BF)
         go(lambda: x_copy(which, k, received_x), which == 2)
@@ -555,7 +606,7 @@
         share_copy(which, k, ref, sib_rows).wait_recv()
 
     barrier = pltpu.get_barrier_semaphore()
-    partners = [sib, xnb, diag] + [dpeer[k] for k in range(1, 8)]
+    partners = list(everyone.values())
     for dev in partners:
         pl.semaphore_signal(barrier, inc=1, device_id=dev, device_id_type=MESH)
     for copy in firsts[0:3]:
@@ -660,34 +711,30 @@
             attend(high[b].astype(F32), b + 2)
             return carry
 
+        wo_send(0)
         ag_step(0, 1, 0)
         lax.fori_loop(0, 2, some, 0)
         ag_step(0, 1, 1)
+        wo_send(1, -1)
         lax.fori_loop(2, 5, some, 0)
         ag_step(0, 2, 0)
         lax.fori_loop(5, 7, some, 0)
         ag_step(0, 2, 1)
+        wo_send(2, -2)
         lax.fori_loop(7, 10, some, 0)
         ag_step(0, 3, 0)
         ag_own(1, 0)
         text_norm()
         ag_step(0, 3, 1)
         ag_own(1, 1)
-        lax.fori_loop(10, 13, some, 0)
+        lax.fori_loop(10, 14, some, 0)
         ag_done(0)
+        wo_send(3, -3, 4)
+        go(lambda: wo_own(lambda: mp))
+        r.wo[mp] = w[0, :, 512:768]
         attention_forward(0)
         ag_step(1, 1, 0)
         attention_forward(1)
-        ar_mid(0, 0, r.cr1, r.xr1)
-        ag_step(1, 1, 1)
-        attention_forward(2)
-        ar_mid(0, 1, r.cr1, r.xr1)
-        ag_step(1, 2, 0)
-        attention_forward(3)
-        ar_mid(0, 2, r.cr1, r.xr1)
-        ag_step(1, 2, 1)
-        lax.fori_loop(13, 14, some, 0)
-        ar_mid(0, 3, r.cr1, r.xr1)
         values = nn(pn[...], iq[2])
         head_all = iota((256, 768), 1) // 64 == iota((256, 768), 0) % 16
         picked = jnp.where(head_all, values, 0.0).astype(BF)
@@ -697,8 +744,7 @@
         after = x0[...] + nn(context, io[...])
         centre, inv = stats(after)
         second = (centre * inv * g2).astype(BF)
-        ag_step(1, 3, 0)
-        ag_own(2, 0)
+        ag_step(1, 1, 1)
         copies[4].wait()
         copies[5].wait()
         leading = after
@@ -710,6 +756,12 @@
         r.emb[mp, y, z] = (leading * norm).astype(BF)
         for k in (1, 2, 3):
             go(partial(emb_copy, k - 1, zpeer[k], lambda: r.emb.at[mp, y, z]), False)
+        attention_forward(2)
+        ag_step(1, 2, 0)
+        attention_forward(3)
+        ag_step(1, 2, 1)
+        ag_step(1, 3, 0)
+        ag_own(2, 0)
 
     def emb_y():
         for k in (1, 2, 3):
@@ -773,8 +825,7 @@
             )
             r.o[at, 0:128] = nn(probs[2], t[3] * hi).astype(BF)
             r.o[at, 128:256] = pair.astype(BF)
-        r.part[rows, :] = nt(r.o[rows, :], w[0, :, 512:768])
-        ar_start(0, k, r.cr1)
+        o_send(k)
 
     def own_alive(k):
         row = r.alive[pl.ds(2 * k + c, 1), :]
@@ -785,14 +836,16 @@
         return jnp.where(iota((16, 256), 1) // 16 == iota((16, 256), 0), row, 0.0).astype(BF)
 
     def second_norm(k):
-        a = r.cap[own_rows(k), :].astype(F32) + ar_end(0, k, r.xr1)
+        o_wait(k)
+        terms = [nt(r.oall[j, k], r.wo[j]) for j in range(4)]
+        a = r.cap[own_rows(k), :].astype(F32) + ((terms[0] + terms[1]) + (terms[2] + terms[3]))
         r.a[k] = a
         centre, inv = stats(a)
         r.n2[own_rows(k), :] = (centre * inv * r.normp[2:3, :] + r.normp[3:4, :]).astype(BF)
         share(0, k, r.n2)
         alive = own_alive(k)
         at = slice(8 * k, 8 * (k + 1))
-        r.asum[at, :] = jnp.dot(alive, a, precision=HIGHEST, preferred_element_type=F32)
+        r.asum[at, :] = nn(jnp.concatenate([alive, alive], axis=1).astype(BF), split(a))
         r.cnt[at, :] = jnp.broadcast_to(jnp.sum(alive, axis=1, keepdims=True), (8, 128))
 
     def mlp_up(k):
@@ -820,6 +873,8 @@
 
     ag_step(1, 3, 1)
     ag_own(2, 1)
+    wo_cores()
+    wo_done()
     second_norm(0)
     ag_done(1)
     ag_step(2, 1, 0)
@@ -945,9 +1000,9 @@
                 dhat - jnp.mean(dhat, axis=-1, keepdims=True)
                 - hat * jnp.mean(dhat * hat, axis=-1, keepdims=True)
             )
-            dout = lax.dot_general(
-                own_alive(k), r.dpc[8 * k : 8 * (k + 1), :], (((0,), (0,)), ((), ())),
-                precision=HIGHEST, preferred_element_type=F32,
+            alive = own_alive(k)
+            dout = tn(
+                jnp.concatenate([alive, alive], axis=0).astype(BF), split(r.dpc[8 * k : 8 * (k + 1), :])
             )
             da = dout + dln
             r.a[k] = da
@@ -1019,11 +1074,11 @@
         r.dh[...] = nn(dy, w[2]).reshape(2, 32, 768)
 
         mlp_backward(0)
+        ar_mid(1, 0, r.cr2, r.xr2)
         mlp_backward(1)
-        ar_mid(1, 0, r.cr2, r.xr2)
         rs_step(2, 1, False)
+        ar_mid(1, 1, r.cr2, r.xr2)
         mlp_backward(2)
-        ar_mid(1, 1, r.cr2, r.xr2)
         rs_step(2, 2, True)
         mlp_backward(3)
         ar_mid(1, 2, r.cr2, r.xr2)
@@ -1168,27 +1223,17 @@
                 else:
                     squares = put(squares, row, 3 + kind, jnp.sum(line, axis=1, keepdims=True))
 
-        sqd, sqm = r.sqd, r.sqm
-
-        def sq_copy(buffer, slot, index, dev):
-            ref = buffer.at[slot()]
-            return rcopy(ref, ref, r.sqs.at[index // 7], r.sqr.at[index], dev)
-
-        sqd[dp] = squares
-        for k in range(1, 8):
-            go(partial(sq_copy, sqd, lambda: dp, k - 1, dpeer[k]), False)
-        for k in range(1, 8):
-            sq_copy(sqd, lambda: (dp - k + 8) % 8, k - 1, dpeer[k]).wait_recv()
-        total = sqd[0]
-        for i in range(1, 8):
-            total = total + sqd[i]
-        sqm[mp] = total
-        others = ((sib, x * 2 + 1 - c), (xnb, (1 - x) * 2 + c), (diag, (1 - x) * 2 + 1 - c))
-        for n, (dev, _) in enumerate(others):
-            go(partial(sq_copy, sqm, lambda: mp, 7 + n, dev), False)
-        for n, (dev, source) in enumerate(others):
-            sq_copy(sqm, lambda: source, 7 + n, dev).wait_recv()
-        r.tot[...] = (sqm[0] + sqm[1]) + (sqm[2] + sqm[3])
+        def sq_copy(k, slot):
+            ref = r.sqd.at[slot]
+            return rcopy(ref, ref, r.sqs.at[0], r.sqr.at[k - 1], everyone[k])
+
+        me = dp * 4 + mp
+        r.sqd[me] = squares
+        for k in range(1, 32):
+            go(partial(sq_copy, k, me), False)
+        for k in range(1, 32):
+            sq_copy(k, (me - k + 32) % 32).wait_recv()
+        r.tot[...] = jnp.sum(r.sqd[...], axis=0)
         final = pltpu.make_async_copy(r.tot, r.tot_o, r.fin.at[4])
         final.start()
         finals.append(final)
@@ -1220,12 +1265,13 @@
         all_sent(w.at[kind, pl.ds(0, 672)], r.ags.at[kind])
         all_sent(r.rss.at[kind], r.rsa.at[kind])
     all_sent(r.n2.at[pl.ds(0, 512)], r.shs.at[0])
+    all_sent(r.wo.at[0], r.wos.at[0])
+    all_sent(r.oall.at[pl.ds(0, 3)], r.oas.at[0])
     all_sent(r.dz.at[pl.ds(0, 512)], r.shs.at[1])
     all_sent(r.a, r.shs.at[2])
     all_sent(r.emb.at[0, 0, pl.ds(0, 3)], r.ems.at[0])
     all_sent(r.gslr.at[pl.ds(0, 7)], r.gss.at[1])
-    all_sent(r.sqd.at[pl.ds(0, 7)], r.sqs.at[0])
-    all_sent(r.sqm.at[pl.ds(0, 3)], r.sqs.at[1])
+    all_sent(r.sqd.at[pl.ds(0, 31)], r.sqs.at[0])
 
 
 def lamb_kernel(*refs):

time: 125 us -> 121 us (0.968)
  Pallas kernels: 124 us -> 120 us
    pallas_call x1, Pallas kernels: 118 us -> 114 us  [fused_shards(): pl.pallas_call(partial(step_kernel, names, total_caps), out_shape=tuple(r...]
where the time goes in v2:
time: 121 us
  Pallas kernels  120 us (99%)
    pallas_call x1, Pallas kernels, fused_shards(): pl.pallas_call(partial(step_kernel, names, total_caps), out_shape=tuple(r...  114 us
    pallas_call x1, Pallas kernels, fused_shards(): pl.pallas_call(lamb_kernel, out_shape=tuple(made) + (jax.ShapeDtypeStruct...  5.99 us

profile of v2, /device:TPU:0, one launch (start us, length us, event | category | flops | bytes accessed | tf_op | source)
XLA Modules:
  0.0 120.5 jit_solution(2227063219283491291)
XLA Ops:
  0.7 113.6 %shard_map.448 = (f32[1024,768]{1,0:T(8,128)}, f32[3,96,768]{2,1,0:T(8,128)}, f32[8,128]{1,0:T(8,128)}, f32[8,128]{1,0:T(8,128)}) custom-call(bf16[1024,768]{1,0:T(8,128)(2,1)} %bitcast.13, s32[16,64]{1,0:T(8,128)} %bitcast.21, s32[1,64]{1,0:T(1,128)} %bitcast.22, bf16[50,2,768]{2,1,0:T(2,128)(2,1)} %bitcast.20, bf16[14,145,768]{2,1,0:T(8,128)(2,1)} %refs_4_.2, ...), custom_call_target="tpu_custom_call" | custom-call | tf_op jit(solution)/shard_map/pallas_call | solution.py:1393
  114.3 6.0 %shard_map.449 = (f32[3,96,192]{2,1,0:T(8,128)}, f32[192,96]{1,0:T(8,128)}, f32[96,768]{1,0:T(8,128)}, f32[96,768]{1,0:T(8,128)}, f32[4,96]{1,0:T(4,128)}, /*ind...) custom-call(f32[3,96,768]{2,1,0:T(8,128)} %get-tuple-element.58.refs, ...), custom_call_target="tpu_custom_call" | custom-call | tf_op jit(solution)/shard_map/pallas_call | solution.py:1407
